TPU v7x, 128 devices: a whole 4x4x4 slice. The times are simulated.
128 devices in a mesh: img: 16 (over z, x), cam: 8 (over y, core).
Axes of the slice: x: 4, y: 4, z: 4, core: 2. Of those that a mesh axis runs over, the one named last changes fastest.
Arguments:
- jac_cam: float32 [49152, 8, 9, 128], P(('img', 'cam')), may hold values from -0.125 to 0.125
- jac_point: float32 [49152, 8, 3, 128], P(('img', 'cam')), may hold values from -0.5 to 0.5
- residual: float32 [49152, 8, 128], P(('img', 'cam')), may hold values from -6 to 6
- obs_count: int32 [49152], P(('img', 'cam')), may hold values from 2 to 8
- obs_camera: int32 [49152, 8], P(('img', 'cam')), may hold values from 0 to 4095
Outputs:
- cam_factor: float32 [45, 4096], P(None, 'cam')
- cam_step: float32 [9, 4096], P(None, 'cam')
- point_step: float32 [3, 49152], P(None, ('img', 'cam'))
All inputs are finite; a program needn't handle non-finite values.
Results may differ from a plain program's by a relative error of at most 0.000076.
Values sent between devices are 32-bit elements; how exact they have to be, the bound alone decides.
A program may use at most 192 MiB of HBM per device.

v0:
```python
import jax
import jax.numpy as jnp
import numpy as np
from jax import lax
from jax.sharding import PartitionSpec as P

CP = 9
CAM_BLK = 512
PACKED = 45


highest = lax.Precision.HIGHEST
lm_lambda = 0.5


def marginalize(jac_cam, jac_point, residual, obs_count):
    slot_count = jac_cam.shape[1]
    live_mask = (jnp.arange(slot_count, dtype=jnp.int32)[None, :] < obs_count[:, None]).astype(
        jac_cam.dtype
    )
    cam_rows = jac_cam * live_mask[:, :, None, None]
    point_rows = jac_point * live_mask[:, :, None, None]
    res_rows = residual * live_mask[:, :, None]

    def inner_product(left, right):
        return jnp.sum(left * right, axis=(1, 2))

    column_zero = point_rows[:, :, 0, :]
    column_one = point_rows[:, :, 1, :]
    column_two = point_rows[:, :, 2, :]
    norm_zero = jnp.sqrt(inner_product(column_zero, column_zero))
    basis_zero = column_zero / norm_zero[:, None, None]
    upper_zero_one = inner_product(basis_zero, column_one)
    remain_one = column_one - upper_zero_one[:, None, None] * basis_zero
    norm_one = jnp.sqrt(inner_product(remain_one, remain_one))
    basis_one = remain_one / norm_one[:, None, None]
    upper_zero_two = inner_product(basis_zero, column_two)
    upper_one_two = inner_product(basis_one, column_two)
    remain_two = (
        column_two
        - upper_zero_two[:, None, None] * basis_zero
        - upper_one_two[:, None, None] * basis_one
    )
    norm_two = jnp.sqrt(inner_product(remain_two, remain_two))
    basis_two = remain_two / norm_two[:, None, None]
    basis_rows = jnp.stack([basis_zero, basis_one, basis_two], axis=2)
    coupling = jnp.einsum("lkpx,lkcx->lkpc", basis_rows, cam_rows, precision=highest)
    reduced_rhs = jnp.einsum("lkpx,lkx->lp", basis_rows, res_rows, precision=highest)
    obs_gram = jnp.einsum("lkcx,lkdx->lkcd", cam_rows, cam_rows, precision=highest) - jnp.einsum(
        "lkpc,lkpd->lkcd", coupling, coupling, precision=highest
    )
    obs_grad = jnp.einsum("lkcx,lkx->lkc", cam_rows, res_rows, precision=highest) - jnp.einsum(
        "lkpc,lp->lkc", coupling, reduced_rhs, precision=highest
    )
    point_factor = (norm_zero, upper_zero_one, upper_zero_two, norm_one, upper_one_two, norm_two)
    return (obs_gram, obs_grad, coupling, reduced_rhs, point_factor)


def point_update(coupling, reduced_rhs, point_factor, camera_table, obs_camera):
    picked = camera_table[obs_camera]
    totals = reduced_rhs + jnp.einsum("lkpc,lkc->lp", coupling, picked, precision=highest)
    norm_zero, upper_zero_one, upper_zero_two, norm_one, upper_one_two, norm_two = point_factor
    solved_two = totals[:, 2] / norm_two
    solved_one = (totals[:, 1] - upper_one_two * solved_two) / norm_one
    solved_zero = (
        totals[:, 0] - upper_zero_one * solved_one - upper_zero_two * solved_two
    ) / norm_zero
    return -jnp.stack([solved_zero, solved_one, solved_two], axis=0)


def pair_positions():
    position = {}
    counter = 0
    for i in range(CP):
        for j in range(i, CP):
            position[i, j] = counter
            counter = counter + 1
    return position


def factor_packed(gram_rows, damping):
    position = pair_positions()
    factor = {}
    for j in range(CP):
        for i in range(j, CP):
            amount = gram_rows[position[j, i]]
            if i == j:
                amount = amount + damping
            for k in range(j):
                amount = amount - factor[k, j] * factor[k, i]
            if i == j:
                factor[j, j] = jnp.sqrt(amount)
            else:
                factor[j, i] = amount / factor[j, j]
    return jnp.stack([factor[i, j] for i in range(CP) for j in range(i, CP)], axis=0)


def camera_solve(packed_factor, gradient):
    position = pair_positions()
    forward = []
    for j in range(CP):
        amount = gradient[j]
        for k in range(j):
            amount = amount - packed_factor[position[k, j]] * forward[k]
        forward.append(amount / packed_factor[position[j, j]])
    backward = [None] * CP
    for i in range(CP - 1, -1, -1):
        amount = forward[i]
        for j in range(i + 1, CP):
            amount = amount - packed_factor[position[i, j]] * backward[j]
        backward[i] = amount / packed_factor[position[i, i]]
    return -jnp.stack(backward, axis=0)


def local(jac_cam, jac_point, residual, obs_count, obs_camera):
    obs_gram, obs_grad, coupling, reduced_rhs, point_factor = marginalize(
        jac_cam, jac_point, residual, obs_count
    )
    flat_index = np.array([i * CP + j for i in range(CP) for j in range(i, CP)], dtype=np.int32)
    packed_rows = obs_gram.reshape(-1, CP * CP)[:, flat_index]
    records = jnp.concatenate([packed_rows, obs_grad.reshape(-1, CP)], axis=1)
    n_cam = lax.axis_size("cam")
    cameras_all = CAM_BLK * n_cam
    partial_sums = jnp.transpose(
        jax.ops.segment_sum(records, obs_camera.reshape(-1), num_segments=cameras_all)
    )
    full = lax.psum(partial_sums, ("img", "cam"))
    block_sums = lax.dynamic_slice_in_dim(full, lax.axis_index("cam") * CAM_BLK, CAM_BLK, 1)
    cam_factor = factor_packed(block_sums[:PACKED], lm_lambda)
    cam_step = camera_solve(cam_factor, block_sums[PACKED:])
    all_steps = lax.all_gather(cam_step, "cam", axis=1, tiled=True)
    point_step = point_update(
        coupling, reduced_rhs, point_factor, jnp.transpose(all_steps), obs_camera
    )
    return (cam_factor, cam_step, point_step)


def solution(mesh):
    in_specs = (
        P(("img", "cam"), None, None, None),
        P(("img", "cam"), None, None, None),
        P(("img", "cam"), None, None),
        P(("img", "cam")),
        P(("img", "cam"), None),
    )
    out_specs = (P(None, "cam"), P(None, "cam"), P(None, ("img", "cam")))
    return jax.shard_map(local, mesh=mesh, in_specs=in_specs, out_specs=out_specs, check_vma=False)
```

profile of v0, /device:TPU:1, one launch (start us, length us, event | category | flops | bytes accessed | tf_op | source)
XLA Modules:
  0.0 536.4 jit_solution(17863167746451550480)
XLA Ops:
  9.0 1.9 broadcast_multiply_fusion.1
  10.9 2.8 copy_multiply_fusion
  14.7 3.9 fusion.9
  18.7 6.0 %multiply_reduce_fusion.1 = f32[384]{0:T(512)S(1)} fusion(f32[384]{0:T(512)S(1)} %fusion.9, f32[384,8,3,128]{3,1,0,2:T(8,128)S(1)} %copy_multiply_fusion, f32[384]{0:T(512)S(1)} %get-tuple-element.143), kind=kLoop, calls=%fused_computation.39 | loop fusion | flops 1965696 | bytes 3150336 | tf_op jit(solution)/shard_map/reduce_sum | solution.py:26
  24.7 10.9 %fusion.13 = (f32[384]{0:T(512)S(1)}, f32[384]{0:T(512)S(1)}) fusion(f32[384,8,3,128]{3,1,0,2:T(8,128)S(1)} %copy_multiply_fusion, f32[384]{0:T(512)S(1)} %get-tuple-element.143, f32[384]{0:T(512)S(1)} %get-tuple-element.141, f32[384]{0:T(512)S(1)} %fusion.9), kind=kLoop, calls=%fused_computation.30 | loop fusion | flops 3144960 | bytes 4726272 | tf_op jit(solution)/shard_map/reduce_sum | solution.py:26
  35.6 7.6 %fusion.17 = f32[384]{0:T(512)S(1)} fusion(f32[384,8,3,128]{3,1,0,2:T(8,128)S(1)} %copy_multiply_fusion, f32[384]{0:T(512)S(1)} %get-tuple-element.16, f32[384]{0:T(512)S(1)} %get-tuple-element.15, f32[384]{0:T(512)S(1)} %get-tuple-element.141, f32[384]{0:T(512)S(1)} %fusion.9, f32[384]{0:T(512)S(1)} %get-tuple-element.143), kind=kLoop, calls=%fused_computation.34 | loop fusion | flops 3931776 | bytes 4727808 | tf_op jit(solution)/shard_map/reduce_sum | solution.py:26
  43.2 5.2 fusion.11
  48.4 11.1 %broadcast_multiply_fusion = f32[384,8,9,128]{3,1,2,0:T(8,128)} fusion(f32[384,8,9,128]{3,1,2,0:T(8,128)} %param.7, f32[384,8]{1,0:T(8,128)S(1)} %fusion.21), kind=kLoop, calls=%fused_computation.10 | loop fusion | flops 3538944 | bytes 28323840 | tf_op jit(solution)/shard_map/mul | solution.py:21
  59.5 50.9 %fusion.4 = f32[384,8,9,9]{3,2,1,0:T(8,128)} fusion(f32[384,8,9,128]{3,1,2,0:T(8,128)} %broadcast_multiply_fusion), kind=kOutput, calls=%fused_computation.7 | convolution fusion | flops 382205952 | bytes 15151104 | tf_op jit(solution)/shard_map/lkcx,lkdx->lkcd/dot_general | solution.py:49
  110.4 40.2 %fusion.2 = f32[384,8,1,9]{3,2,1,0:T(1,128)S(1)} fusion(f32[384,8,128,1]{2,3,1,0:T(1,128)S(1)} %bitcast.107, f32[384,8,9,128]{3,1,2,0:T(8,128)S(1)} %copy-done), kind=kOutput, calls=%fused_computation.5 | convolution fusion | flops 42467328 | bytes 15839232 | tf_op jit(solution)/shard_map/lkcx,lkx->lkc/dot_general | solution.py:52
  151.0 2.1 copy-done.1
  153.1 25.8 %fusion.6 = f32[384,1,3,1]{2,1,3,0:T(1,128)S(1)} fusion(f32[384,8,128,1]{2,3,1,0:T(1,128)S(1)} %bitcast.108, f32[384,8,3,128]{3,1,2,0:T(8,128)S(1)} %pad_maximum_fusion), kind=kOutput, calls=%fused_computation.11 | convolution fusion | flops 14155776 | bytes 6296064 | tf_op jit(solution)/shard_map/lkpx,lkx->lp/dot_general | solution.py:48
  179.2 46.7 %multiply_reduce_fusion = (f32[384,8,9]{2,1,0:T(8,128)S(1)}, f32[384,8,3,9]{3,2,1,0:T(4,128)}) fusion(f32[384,3]{1,0:T(8,128)S(1)} %copy.243, f32[384,8,9,128]{3,1,2,0:T(8,128)} %broadcast_multiply_fusion, f32[384,8,3,128]{3,1,2,0:T(8,128)} %copy-done.1), kind=kOutput, calls=%fused_computation.14 | convolution fusion | flops 127540224 | bytes 19321344 | tf_op jit(solution)/shard_map/lkpx,lkcx->lkpc/dot_general | solution.py:47
  225.9 3.5 copy.237
  229.4 4.4 copy.231
  233.8 2.2 bitcast_subtract_fusion
  237.0 45.2 %convolution_subtract_fusion = f32[384,8,9,9]{3,2,1,0:T(8,128)} fusion(f32[384,8,9,9]{3,2,1,0:T(8,128)} %fusion.4, f32[384,8,3,9]{3,2,1,0:T(4,128)} %get-tuple-element.177), kind=kOutput, calls=%fused_computation.9 | convolution fusion | flops 9206784 | bytes 2322432 | tf_op jit(solution)/shard_map/lkpc,lkpd->lkcd/dot_general | solution.py:49
  282.2 14.6 %reshape.214 = f32[3072,81]{1,0:T(8,128)S(1)} reshape(f32[384,8,9,9]{3,2,1,0:T(8,128)} %convolution_subtract_fusion) | data formatting | bytes 1990656 | tf_op jit(solution)/shard_map/reshape | solution.py:120
  300.0 18.0 %scatter_custom_fusion = f32[4096,54]{1,0:T(8,128)S(1)} fusion(s32[3072]{0:T(1024)S(1)} %reshape.198, f32[3072,54]{1,0:T(8,128)} %copy.226, f32[]{:T(128)} %constant.9.clone.1), kind=kCustom, calls=%fused_computation.40 | custom fusion | flops 165888 | bytes 885248 | tf_op jit(solution)/shard_map/scatter-add | solution.py:125
  319.9 149.9 %all-reduce.2.cloned.1.call-done = f32[54,4096]{1,0:T(8,128)} async-done(((f32[54,4096]{1,0:T(8,128)}), f32[54,4096]{1,0:T(8,128)}) %all-reduce.2.cloned.1.call-update) | async-done | bytes 884752 | tf_op jit(solution)/shard_map/psum | solution.py:127
  474.0 13.2 %all_gather.3 = f32[9,4096]{1,0:T(8,128)S(1)} all-gather(f32[9,512]{1,0:T(8,128)S(1)} %neg.6), channel_id=1, replica_groups=mesh['img'=16,'cam'=8] {'cam'}, dimensions={1}, use_global_device_ids=true | all-gather | bytes 165888 | tf_op jit(solution)/shard_map/all_gather | solution.py:131
  487.8 10.8 %gather_fusion.1 = f32[3072,9]{1,0:T(8,128)} fusion(f32[4096,9]{1,0:T(8,128)S(1)} %copy.229, s32[3072]{0:T(1024)S(1)} %broadcast_clamp_fusion), kind=kCustom, calls=%fused_computation.1 | custom fusion | bytes 233472 | tf_op jit(solution)/shard_map/gather | solution.py:60
  498.6 24.9 %fusion.129 = f32[384,1,3,1]{2,1,3,0:T(1,128)S(1)} fusion(f32[384,8,3,9]{3,2,1,0:T(4,128)} %get-tuple-element.177, f32[384,8,9,1]{2,3,1,0:T(1,128)} %bitcast.111), kind=kOutput, calls=%fused_computation.277 | convolution fusion | flops 995328 | bytes 446976 | tf_op jit(solution)/shard_map/lkpc,lkc->lp/dot_general | solution.py:61
  525.5 3.8 stack.9
  (53 shorter events, 16.1 us)
Async XLA Ops:
  7.2 462.7 %all-reduce.2.cloned.1.call-start = ((), (), s32[]{:S(2)}) async-start(), calls=%async_computation | async-start | bytes 1835008 | tf_op jit(solution)/shard_map/psum | solution.py:127
  59.5 51.0 %copy-start = (f32[384,8,9,128]{3,1,2,0:T(8,128)S(1)}, f32[384,8,9,128]{3,1,2,0:T(8,128)}, u32[]{:S(2)}) copy-start(f32[384,8,9,128]{3,1,2,0:T(8,128)} %broadcast_multiply_fusion) | copy-start | bytes 42467332
  110.4 40.2 %copy-start.2 = (f32[384,8,1,128]{3,1,2,0:T(8,128)S(1)}, f32[384,8,1,128]{3,1,2,0:T(8,128)}, u32[]{:S(2)}) copy-start(f32[384,8,1,128]{3,1,2,0:T(8,128)} %get-tuple-element.126) | copy-start | bytes 4718596
  110.4 40.2 %copy-start.3 = (f32[384,8,1,128]{3,1,2,0:T(8,128)S(1)}, f32[384,8,1,128]{3,1,2,0:T(8,128)}, u32[]{:S(2)}) copy-start(f32[384,8,1,128]{3,1,2,0:T(8,128)} %get-tuple-element.127) | copy-start | bytes 4718596
  110.4 40.3 %copy-start.4 = (f32[384,8,1,128]{3,1,2,0:T(8,128)S(1)}, f32[384,8,1,128]{3,1,2,0:T(8,128)}, u32[]{:S(2)}) copy-start(f32[384,8,1,128]{3,1,2,0:T(8,128)} %get-tuple-element.128) | copy-start | bytes 4718596
  151.0 2.1 copy-start.1
  296.9 0.7 copy-start.7
  318.0 1.6 copy-start.6
  474.0 24.7 %copy-start.5 = (f32[9,512]{1,0:T(8,128)}, f32[9,512]{1,0:T(8,128)S(1)}, u32[]{:S(2)}) copy-start(f32[9,512]{1,0:T(8,128)S(1)} %neg.6) | copy-start | bytes 55300
Sparse Core Ops, SparseCore 0:
  319.7 150.0 all-reduce.1
where the time goes:
time: 544 us; the launch traced here: 536 us
  matrix products  234 us (43%)
  waiting for transfers between devices  150 us (28%)
  other arithmetic  77.6 us (14%)
  local copies, waits for them, and re-layouts  47.2 us (9%)
  between operations  14.5 us (3%)
  blocking collectives  13.2 us (2%)
    psum x1, waiting for transfers between devices, local(): full = lax.psum(partial_sums, ('img', 'cam'))  150 us
    dot_general x1, matrix products, marginalize(): jnp.einsum('lkcx,lkdx->lkcd', cam_rows, cam_rows, precision=highest)  50.9 us
    dot_general x1, matrix products, marginalize(): jnp.einsum('lkpx,lkcx->lkpc', basis_rows, cam_rows, precision=highest)  46.7 us
    dot_general x1, matrix products, marginalize(): jnp.einsum('lkpc,lkpd->lkcd', coupling, coupling, precision=highest)  45.2 us
    dot_general x1, matrix products, marginalize(): jnp.einsum('lkcx,lkx->lkc', cam_rows, res_rows, precision=highest)  40.2 us
    reduce_sum x5, other arithmetic, inner_product(): return jnp.sum(left * right, axis=(1, 2))  29.4 us
    dot_general x1, matrix products, marginalize(): jnp.einsum('lkpx,lkx->lp', basis_rows, res_rows, precision=highest)  25.8 us
    dot_general x1, matrix products, point_update(): jnp.einsum('lkpc,lkc->lp', coupling, picked, precision=highest)  24.9 us
  transfers between devices with their start and end apart: 1, of which 1 were waited for; matrix products, arithmetic and copies ran while one was open for 0% of the time, Pallas kernels for 0%

commit v1 on v0

v1 whole, which is shorter than its diff:
```python
import functools

import jax
import jax.numpy as jnp
from jax import lax
from jax.experimental import pallas as pl
from jax.experimental.pallas import tpu as pltpu
from jax.sharding import PartitionSpec as P

CP = 9
K = 8
NL = 384
NB = 3
NOBS = NL * K
PACKED = 45
ROWS = 56
NIMG = 16
NY = 4
LM_LAMBDA = 0.5
f32 = jnp.float32
bf16 = jnp.bfloat16
MESH = pl.DeviceIdType.MESH

CC = [(i, j) for i in range(CP) for j in range(i, CP)]
CR = [(i, 9) for i in range(CP)]
QC = [(10 + p, c) for p in range(3) for c in range(CP)]
QR = [(10 + p, 9) for p in range(3)]
PAIRS = CC + CR + QC + QR
GROUPS = [PAIRS[0:28], PAIRS[28:56], PAIRS[56:84]]


def marginalize_kernel(
    jc, jp, rs, cnt, cam, rec_out, coup_out, small_out, cam_out,
    jcv, jpv, rsv, qt, ta, tb, acc, rec, sem,
):
    def copy(b, which):
        s = pl.ds(b * 128, 128)
        src, dst = ((jp, jpv), (jc, jcv), (rs, rsv))[which]
        return pltpu.make_async_copy(src.at[s], dst.at[s], sem.at[b, which])

    for which in range(3):
        for b in range(NB):
            copy(b, which).start()

    jcf = jcv.reshape(NL * CP * K, 128)
    jpf = jpv.reshape(NL * 3 * K, 128)
    rsf = rsv.reshape(NL * K, 128)

    for b in range(NB):
        for k in range(K):
            cam_out[0:1, (b * K + k) * 128 : (b * K + k + 1) * 128] = cam[k : k + 1, b * 128 : (b + 1) * 128]

    def point_phase(b, _):
        copy(b, 0).wait()
        count = cnt[pl.ds(b, 1), :]
        zero = jnp.zeros((8, 128), f32)

        def first(k, sums):
            live = (count > k).astype(f32)
            parts = []
            for p in range(3):
                v = jpf[pl.ds(b * (128 * 3 * K) + p * K + k, 128, stride=3 * K), :].T * live
                qt[p, b * K + k] = v
                parts.append(v)
            sums = list(sums)
            for x in range(16):
                a = [v[8 * x : 8 * x + 8] for v in parts]
                for q in range(3):
                    sums[q] = sums[q] + a[0] * a[q]
            return tuple(sums)

        s00, s01, s02 = [
            jnp.sum(v, axis=0, keepdims=True) for v in lax.fori_loop(0, K, first, (zero,) * 3)
        ]
        norm0 = jnp.sqrt(s00)
        inv0 = 1.0 / norm0
        r01 = s01 * inv0
        r02 = s02 * inv0
        c01 = r01 * inv0
        c02 = r02 * inv0

        def second(k, sums):
            n1, s12 = sums
            for x in range(16):
                rows = pl.ds(8 * x, 8)
                rem = qt[1, b * K + k, rows, :] - c01 * qt[0, b * K + k, rows, :]
                qt[1, b * K + k, rows, :] = rem
                n1 = n1 + rem * rem
                s12 = s12 + rem * qt[2, b * K + k, rows, :]
            return n1, s12

        n11, s12 = [
            jnp.sum(v, axis=0, keepdims=True) for v in lax.fori_loop(0, K, second, (zero,) * 2)
        ]
        norm1 = jnp.sqrt(n11)
        inv1 = 1.0 / norm1
        r12 = s12 * inv1
        c12 = r12 * inv1

        def third(k, n2):
            for x in range(16):
                rows = pl.ds(8 * x, 8)
                rem = (
                    qt[2, b * K + k, rows, :]
                    - c02 * qt[0, b * K + k, rows, :]
                    - c12 * qt[1, b * K + k, rows, :]
                )
                qt[2, b * K + k, rows, :] = rem
                n2 = n2 + rem * rem
            return n2

        n22 = jnp.sum(lax.fori_loop(0, K, third, zero), axis=0, keepdims=True)
        norm2 = jnp.sqrt(n22)
        inv2 = 1.0 / norm2
        for n, v in enumerate((inv0, inv1, inv2, r01, r02, r12)):
            small_out[b, n : n + 1, :] = v
        return 0

    lax.fori_loop(0, NB, point_phase, 0)

    def turn(b, k, t):
        for c in range(CP):
            t[c] = jcf[pl.ds(b * (128 * CP * K) + c * K + k, 128, stride=CP * K), :].T
        t[9] = rsf[pl.ds(b * (128 * K) + k, 128, stride=K), :].T

    def products(b, k, t):
        base = 0
        for pairs in GROUPS:
            total = [None] * len(pairs)
            for x in range(16):
                rows = pl.ds(8 * x, 8)
                held = {}
                for n, pair in enumerate(pairs):
                    for q in pair:
                        if q not in held:
                            held[q] = t[q, rows, :] if q < 10 else qt[q - 10, b * K + k, rows, :]
                    term = held[pair[0]] * held[pair[1]]
                    total[n] = term if total[n] is None else total[n] + term
            for n in range(len(pairs)):
                acc[base + n, pl.ds(pl.multiple_of(k * 8, 8), 8), :] = total[n]
            base += len(pairs)

    def camera_phase(b, _):
        copy(b, 1).wait()
        copy(b, 2).wait()
        turn(b, 0, ta)

        def two(h, _):
            turn(b, 2 * h + 1, tb)
            products(b, 2 * h, ta)
            turn(b, jnp.minimum(2 * h + 2, K - 1), ta)
            products(b, 2 * h + 1, tb)
            return 0

        lax.fori_loop(0, K // 2, two, 0)

        def entry(n):
            v = acc[n, pl.ds(0, 8, stride=8), :]
            for s in range(1, 8):
                v = v + acc[n, pl.ds(s, 8, stride=8), :]
            return v

        slot = lax.broadcasted_iota(jnp.int32, (8, 128), 0)
        live = (slot < cnt[pl.ds(b, 1), :]).astype(f32)
        inv = [small_out[b, p : p + 1, :] for p in range(3)]
        coupling = [[entry(54 + p * CP + c) * inv[p] for c in range(CP)] for p in range(3)]
        for p in range(3):
            for c in range(CP):
                coup_out[b, p * CP + c] = coupling[p][c]
        rhs = [jnp.sum(entry(81 + p), axis=0, keepdims=True) * inv[p] for p in range(3)]
        for p in range(3):
            small_out[b, 6 + p : 7 + p, :] = rhs[p]
        for n, (i, j) in enumerate(CC):
            v = entry(n) * live
            for p in range(3):
                v = v - coupling[p][i] * coupling[p][j]
            rec[n * 8 : n * 8 + 8, :] = v
        for i in range(CP):
            v = entry(45 + i) * live
            for p in range(3):
                v = v - coupling[p][i] * rhs[p]
            rec[(45 + i) * 8 : (45 + i) * 8 + 8, :] = v
        for i in range(54, ROWS):
            rec[i * 8 : i * 8 + 8, :] = jnp.zeros((8, 128), f32)
        for k in range(K):
            v = rec[pl.ds(k, ROWS, stride=8), :]
            high = v.astype(bf16).astype(f32)
            both = jnp.concatenate([high, v - high], axis=0).astype(bf16)
            rec_out[:, pl.ds(pl.multiple_of((b * K + k) * 128, 128), 128)] = both
        return 0

    lax.fori_loop(0, NB, camera_phase, 0)


def marginalize(jac_cam, jac_point, residual, count, cam):
    hbm = pl.BlockSpec(memory_space=pltpu.MemorySpace.HBM)
    vmem = pl.BlockSpec(memory_space=pltpu.MemorySpace.VMEM)
    return pl.pallas_call(
        marginalize_kernel,
        out_shape=(
            jax.ShapeDtypeStruct((2 * ROWS, NOBS), bf16),
            jax.ShapeDtypeStruct((NB, 27, 8, 128), f32),
            jax.ShapeDtypeStruct((NB, 16, 128), f32),
            jax.ShapeDtypeStruct((1, NOBS), jnp.int32),
        ),
        in_specs=[hbm, hbm, hbm, vmem, vmem],
        out_specs=(vmem,) * 4,
        scratch_shapes=[
            pltpu.VMEM((NL, CP, K, 128), f32),
            pltpu.VMEM((NL, 3, K, 128), f32),
            pltpu.VMEM((NL, K, 128), f32),
            pltpu.VMEM((3, NB * K, 128, 128), f32),
            pltpu.VMEM((10, 128, 128), f32),
            pltpu.VMEM((10, 128, 128), f32),
            pltpu.VMEM((len(PAIRS), 64, 128), f32),
            pltpu.VMEM((ROWS * 8, 128), f32),
            pltpu.SemaphoreType.DMA((NB, 3)),
        ],
        compiler_params=pltpu.CompilerParams(vmem_limit_bytes=52 << 20),
        cost_estimate=pl.CostEstimate(flops=70_000_000, bytes_accessed=21_000_000, transcendentals=0),
        name="marginalize",
    )(jac_cam, jac_point, residual, count, cam)


def pair_positions():
    position = {}
    for i in range(CP):
        for j in range(i, CP):
            position[i, j] = len(position)
    return position


def camera_solve(load):
    position = pair_positions()
    factor, inverse = {}, []
    for j in range(CP):
        for i in range(j, CP):
            amount = load(position[j, i])
            if i == j:
                amount = amount + LM_LAMBDA
            for k in range(j):
                amount = amount - factor[k, j] * factor[k, i]
            if i == j:
                factor[j, j] = jnp.sqrt(amount)
                inverse.append(1.0 / factor[j, j])
            else:
                factor[j, i] = amount * inverse[j]
    forward = []
    for j in range(CP):
        amount = load(PACKED + j)
        for k in range(j):
            amount = amount - factor[k, j] * forward[k]
        forward.append(amount * inverse[j])
    backward = [None] * CP
    for i in range(CP - 1, -1, -1):
        amount = forward[i]
        for j in range(i + 1, CP):
            amount = amount - factor[i, j] * backward[j]
        backward[i] = amount * inverse[i]
    return [factor[i, j] for i in range(CP) for j in range(i, CP)], [-v for v in backward]


def fill_onehot(cam, onehot):
    for t in range(NOBS // 256):
        lane = cam[0:1, t * 256 : (t + 1) * 256] & 255
        hit = lax.broadcasted_iota(jnp.int32, (256, 256), 0) == lane
        onehot[:, t * 256 : (t + 1) * 256] = hit.astype(f32).astype(bf16)


def camera_kernel(
    rec, cam, fac_out, steps,
    onehot, lhs, away, home, from_core, from_y, block, from_img, full, spread,
    send_a, recv_a, send_b, recv_b, send_c, recv_c, send_d, recv_d, send_e, recv_e,
):
    img, mine = lax.axis_index("img"), lax.axis_index("cam")
    y, core = mine // 2, mine % 2

    barrier = pltpu.get_barrier_semaphore()
    for d in range(1, NIMG):
        pl.semaphore_signal(barrier, inc=1, device_id=((img + d) % NIMG, mine), device_id_type=MESH)
    for d in range(1, 8):
        pl.semaphore_signal(barrier, inc=1, device_id=(img, (mine + d) % 8), device_id_type=MESH)

    fill_onehot(cam, onehot)

    def sums_of(owner):
        for half in range(2):
            for t in range(6):
                cols = slice(t * 512, (t + 1) * 512)
                hit = (cam[0:1, cols] >> 8) == owner * 2 + half
                mask = jnp.broadcast_to(hit.astype(f32), (16, 512)).astype(bf16)
                mask = jnp.concatenate([mask] * 7, axis=0)
                lhs[half * 112 : (half + 1) * 112, cols] = rec[:, cols] * mask
        r = lax.dot_general(
            lhs[...], onehot[...], (((1,), (1,)), ((), ())), preferred_element_type=f32
        )
        return [r[112 * h : 112 * h + 56] + r[112 * h + 56 : 112 * h + 112] for h in range(2)]

    to_core = []
    for d in range(4):
        to_y = (y + 2 - d + 4) % 4
        sums = sums_of(to_y * 2 + 1 - core)
        for h in range(2):
            away[d, h] = sums[h]
        if d == 0:
            pl.semaphore_wait(barrier, 22)
        copy = pltpu.make_async_remote_copy(
            src_ref=away.at[d], dst_ref=from_core.at[d], send_sem=send_a.at[d], recv_sem=recv_a.at[d],
            device_id=(img, y * 2 + 1 - core), device_id_type=MESH,
        )
        copy.start()
        to_core.append(copy)

    to_ys = []
    for d in range(4):
        away_by = (2 - d + 4) % 4
        to_y = (y + away_by) % 4
        sums = sums_of(to_y * 2 + core)
        to_core[d].wait_recv()
        for h in range(2):
            home[d, h] = sums[h] + from_core[d, h]
        if away_by:
            copy = pltpu.make_async_remote_copy(
                src_ref=home.at[d], dst_ref=from_y.at[away_by - 1],
                send_sem=send_b.at[away_by - 1], recv_sem=recv_b.at[away_by - 1],
                device_id=(img, to_y * 2 + core), device_id_type=MESH,
            )
            copy.start()
            to_ys.append(copy)
    own = 2
    for copy in to_ys:
        copy.wait_recv()
    for h in range(2):
        total = home[own, h] + from_y[0, h] + from_y[1, h] + from_y[2, h]
        for r in range(7):
            block[h * 7 + r] = total[8 * r : 8 * r + 8]

    def slice_copy(d):
        return pltpu.make_async_remote_copy(
            src_ref=block.at[(img + d) % NIMG], dst_ref=from_img.at[d],
            send_sem=send_c.at[d], recv_sem=recv_c.at[d],
            device_id=((img + d) % NIMG, mine), device_id_type=MESH,
        )

    for d in range(1, NIMG):
        @pl.when((img + d) % NIMG < 14)
        def _(d=d):
            slice_copy(d).start()

    def sum_copy(d):
        return pltpu.make_async_remote_copy(
            src_ref=full.at[img], dst_ref=full.at[img],
            send_sem=send_d.at[d], recv_sem=recv_d.at[d],
            device_id=((img + d) % NIMG, mine), device_id_type=MESH,
        )

    @pl.when(img < 14)
    def _():
        for d in range(1, NIMG):
            slice_copy(d).wait_recv()
        total = block[img]
        for d in range(1, NIMG):
            total = total + from_img[d]
        full[img] = total
        for d in range(1, NIMG):
            sum_copy(d).start()

    for d in range(1, NIMG):
        @pl.when((img - d + NIMG) % NIMG < 14)
        def _(d=d):
            sum_copy(d).wait_recv()

    for h in range(2):
        for r in range(7):
            for e in range(2):
                spread[pl.ds(r * 32 + h * 2 + e, 8, stride=4), :] = full[h * 7 + r, :, e * 128 : (e + 1) * 128]
    factor, step = camera_solve(lambda c: spread[4 * c : 4 * c + 4, :])
    for n, v in enumerate(factor):
        for q in range(4):
            fac_out[n : n + 1, q * 128 : (q + 1) * 128] = v[q : q + 1]
    steps[mine] = jnp.zeros((2, 16, 256), f32)
    for n, v in enumerate(step):
        for q in range(4):
            steps[mine, q // 2, n : n + 1, (q % 2) * 128 : (q % 2 + 1) * 128] = v[q : q + 1]

    to_cams = []
    for d in range(1, 8):
        copy = pltpu.make_async_remote_copy(
            src_ref=steps.at[mine], dst_ref=steps.at[mine],
            send_sem=send_e.at[d], recv_sem=recv_e.at[d],
            device_id=(img, (mine + d) % 8), device_id_type=MESH,
        )
        copy.start()
        to_cams.append(copy)

    for copy in to_core + to_ys:
        copy.wait_send()
    for d in range(1, NIMG):
        @pl.when((img + d) % NIMG < 14)
        def _(d=d):
            slice_copy(d).wait_send()

    @pl.when(img < 14)
    def _():
        for d in range(1, NIMG):
            sum_copy(d).wait_send()

    for copy in to_cams:
        copy.wait_recv()
    for copy in to_cams:
        copy.wait_send()


def camera_update(records, cam):
    vmem = pl.BlockSpec(memory_space=pltpu.MemorySpace.VMEM)
    dma = pltpu.SemaphoreType.DMA
    return pl.pallas_call(
        camera_kernel,
        out_shape=(
            jax.ShapeDtypeStruct((PACKED, 512), f32),
            jax.ShapeDtypeStruct((8, 2, 16, 256), f32),
        ),
        in_specs=[vmem, vmem],
        out_specs=(vmem, vmem),
        scratch_shapes=[
            pltpu.VMEM((256, NOBS), bf16),
            pltpu.VMEM((224, NOBS), bf16),
            pltpu.VMEM((4, 2, ROWS, 256), f32),
            pltpu.VMEM((4, 2, ROWS, 256), f32),
            pltpu.VMEM((4, 2, ROWS, 256), f32),
            pltpu.VMEM((3, 2, ROWS, 256), f32),
            pltpu.VMEM((NIMG, 8, 256), f32),
            pltpu.VMEM((NIMG, 8, 256), f32),
            pltpu.VMEM((NIMG, 8, 256), f32),
            pltpu.VMEM((ROWS * 4, 128), f32),
            dma((4,)), dma((4,)), dma((3,)), dma((3,)), dma((NIMG,)), dma((NIMG,)),
            dma((NIMG,)), dma((NIMG,)), dma((8,)), dma((8,)),
        ],
        compiler_params=pltpu.CompilerParams(
            collective_id=0, has_side_effects=True, vmem_limit_bytes=40 << 20
        ),
        name="camera_update",
    )(records, cam)


def point_kernel(fac, steps, cam, coup, small, fac_out, step_out, point_out, onehot, picked):
    mine = lax.axis_index("cam")
    fac_out[...] = fac[...]
    for h in range(2):
        step_out[:, h * 256 : (h + 1) * 256] = steps[mine, h, 0:CP, :]
    fill_onehot(cam, onehot)
    table = steps[...].reshape(256, 256)
    high = table.astype(bf16)
    low = (table - high.astype(f32)).astype(bf16)
    for b in range(NB):
        for q in range(4):
            cols = slice(b * 1024 + q * 256, b * 1024 + (q + 1) * 256)
            chosen = jnp.dot(high, onehot[:, cols], preferred_element_type=f32) + jnp.dot(
                low, onehot[:, cols], preferred_element_type=f32
            )
            group = cam[0:1, cols] >> 8
            total = jnp.zeros((16, 256), f32)
            for g in range(16):
                total = total + jnp.where(group == g, chosen[16 * g : 16 * g + 16], 0.0)
            for e in range(2):
                picked[pl.ds(q * 2 + e, 16, stride=8), :] = total[:, e * 128 : (e + 1) * 128]
        sums = []
        for p in range(3):
            v = coup[b, p * CP] * picked[0:8, :]
            for c in range(1, CP):
                v = v + coup[b, p * CP + c] * picked[c * 8 : c * 8 + 8, :]
            sums.append(small[b, 6 + p : 7 + p, :] + jnp.sum(v, axis=0, keepdims=True))
        inv = [small[b, p : p + 1, :] for p in range(3)]
        r01, r02, r12 = [small[b, p : p + 1, :] for p in range(3, 6)]
        two = sums[2] * inv[2]
        one = (sums[1] - r12 * two) * inv[1]
        zero = (sums[0] - r01 * one - r02 * two) * inv[0]
        for p, v in enumerate((zero, one, two)):
            point_out[p : p + 1, b * 128 : (b + 1) * 128] = -v


def point_update(fac, steps, cam, coup, small):
    vmem = pl.BlockSpec(memory_space=pltpu.MemorySpace.VMEM)
    return pl.pallas_call(
        point_kernel,
        out_shape=(
            jax.ShapeDtypeStruct((PACKED, 512), f32),
            jax.ShapeDtypeStruct((CP, 512), f32),
            jax.ShapeDtypeStruct((3, NL), f32),
        ),
        in_specs=[vmem] * 5,
        out_specs=(vmem,) * 3,
        scratch_shapes=[pltpu.VMEM((256, NOBS), bf16), pltpu.VMEM((128, 128), f32)],
        compiler_params=pltpu.CompilerParams(vmem_limit_bytes=32 << 20),
        name="point_update",
    )(fac, steps, cam, coup, small)


def local(jac_cam, jac_point, residual, obs_count, obs_camera):
    records, coup, small, cam = marginalize(
        jnp.transpose(jac_cam, (0, 2, 1, 3)),
        jnp.transpose(jac_point, (0, 2, 1, 3)),
        residual,
        obs_count.reshape(NB, 128),
        jnp.transpose(obs_camera),
    )
    fac, steps = camera_update(records, cam)
    return point_update(fac, steps, cam, coup, small)


def solution(mesh):
    in_specs = (
        P(("img", "cam"), None, None, None),
        P(("img", "cam"), None, None, None),
        P(("img", "cam"), None, None),
        P(("img", "cam")),
        P(("img", "cam"), None),
    )
    out_specs = (P(None, "cam"), P(None, "cam"), P(None, ("img", "cam")))
    return jax.shard_map(local, mesh=mesh, in_specs=in_specs, out_specs=out_specs, check_vma=False)
```

time: 544 us -> 59.1 us (0.11); the launches traced: 536 us -> 58.9 us
  matrix products: 234 us -> 0 us
  waiting for transfers between devices: 150 us -> 0 us
  other arithmetic: 77.6 us -> 0 us
  Pallas kernels: 0 us -> 56.8 us
  local copies, waits for them, and re-layouts: 47.2 us -> 1.38 us
  between operations: 14.5 us -> 0.66 us
  blocking collectives: 13.2 us -> 0 us
    dot_general x6 -> x0, matrix products: 234 us -> none  [the longest x1 50.9 us: marginalize(): jnp.einsum('lkcx,lkdx->lkcd', cam_rows, cam_rows, precision=highest)]
    psum x1 -> x0, waiting for transfers between devices: 150 us -> none  [local(): full = lax.psum(partial_sums, ('img', 'cam'))]
    pallas_call x0 -> x3, Pallas kernels: none -> 56.8 us  [the longest x1 35.4 us: camera_update(): pl.pallas_call(camera_kernel, out_shape=(jax.ShapeDtypeStruct((PACKED, 51...]
    reduce_sum x5 -> x0, other arithmetic: 29.4 us -> none  [inner_product(): return jnp.sum(left * right, axis=(1, 2))]
    scatter-add x1 -> x0, other arithmetic: 18 us -> none  [local(): jax.ops.segment_sum(records, obs_camera.reshape(-1), num_segments=cameras...]
    reshape x3 -> x0, local copies, waits for them, and re-layouts: 16.2 us -> none  [the longest x2 15.2 us: local(): packed_rows = obs_gram.reshape(-1, CP * CP)[:, flat_index]]
    mul x3 -> x0, other arithmetic: 15.8 us -> none  [the longest x1 11.1 us: marginalize(): cam_rows = jac_cam * live_mask[:, :, None, None]]
    all_gather x1 -> x0, blocking collectives: 13.2 us -> none  [local(): all_steps = lax.all_gather(cam_step, 'cam', axis=1, tiled=True)]
  transfers between devices with their start and end apart: 1 -> 0, of which waited for: 1 -> 0; matrix products, arithmetic and copies ran while one was open for 0% -> 0% of each run, Pallas kernels for 0% -> 0%
where the time goes in v1:
time: 59.1 us; the launch traced here: 58.9 us
  Pallas kernels  56.8 us (96%)
  local copies, waits for them, and re-layouts  1.38 us (2%)
  between operations  0.66 us (1%)
    pallas_call x1, Pallas kernels, camera_update(): pl.pallas_call(camera_kernel, out_shape=(jax.ShapeDtypeStruct((PACKED, 51...  35.4 us
    pallas_call x1, Pallas kernels, marginalize(): pl.pallas_call(marginalize_kernel, out_shape=(jax.ShapeDtypeStruct((2 * R...  19.4 us
    pallas_call x1, Pallas kernels, point_update(): pl.pallas_call(point_kernel, out_shape=(jax.ShapeDtypeStruct((PACKED, 512...  2.04 us
    unnamed x4, local copies, waits for them, and re-layouts  1.38 us

profile of v1, /device:TPU:1, one launch (start us, length us, event | category | flops | bytes accessed | tf_op | source)
XLA Modules:
  0.0 58.9 jit_solution(10830081831551003622)
XLA Ops:
  0.6 0.0 copy-start
  0.6 0.7 %copy-done = s32[384,8]{0,1:T(8,128)S(1)} copy-done((s32[384,8]{0,1:T(8,128)S(1)}, s32[384,8]{0,1:T(8,128)}, u32[]{:S(2)}) %copy-start) | copy-done | bytes 12312
  1.3 0.0 copy-start.1
  1.3 0.7 %copy-done.1 = s32[384]{0:T(512)S(1)} copy-done((s32[384]{0:T(512)S(1)}, s32[384]{0:T(512)}, u32[]{:S(2)}) %copy-start.1) | copy-done | bytes 1560
  2.0 19.4 %marginalize.1 = (bf16[112,3072]{1,0:T(8,128)(2,1)S(1)}, f32[3,27,8,128]{3,2,1,0:T(8,128)S(1)}, f32[3,16,128]{2,1,0:T(8,128)S(1)}, s32[1,3072]{1,0:T(1,128)S(1)}) custom-call(f32[384,9,8,128]{3,2,1,0:T(8,128)} %bitcast.6, f32[384,3,8,128]{3,2,1,0:T(8,128)} %bitcast.7, f32[384,8,128]{2,1,0:T(8,128)} %rs.1, s32[3,128]{1,0:T(4,128)S(1)} %bitcast.5, ...), custom_call_target="tpu_custom_call" | custom-call | flops 70000000 | bytes 21000000 | tf_op jit(solution)/shard_map/marginalize/pallas_call | solution.py:198
  21.4 35.4 %camera_update.1 = (f32[45,512]{1,0:T(8,128)S(1)}, f32[8,2,16,256]{3,2,1,0:T(8,128)S(1)}) custom-call(bf16[112,3072]{1,0:T(8,128)(2,1)S(1)} %get-tuple-element.9.rec, s32[1,3072]{1,0:T(1,128)S(1)} %get-tuple-element.10.cam), custom_call_target="tpu_custom_call" | custom-call | tf_op jit(solution)/shard_map/camera_update/pallas_call | solution.py:417
  56.8 2.0 %point_update.1 = (f32[45,512]{1,0:T(8,128)}, f32[9,512]{1,0:T(8,128)}, f32[3,384]{1,0:T(4,128)}) custom-call(f32[45,512]{1,0:T(8,128)S(1)} %get-tuple-element.11.fac, f32[8,2,16,256]{3,2,1,0:T(8,128)S(1)} %get-tuple-element.12.steps, s32[1,3072]{1,0:T(1,128)S(1)} %get-tuple-element.10.cam, f32[3,27,8,128]{3,2,1,0:T(8,128)S(1)} %get-tuple-element.13.coup, ...), custom_call_target="tpu_custom_call" | custom-call | tf_op jit(solution)/shard_map/point_update/pallas_call | solution.py:484
Async XLA Ops:
  0.6 0.7 %copy-start = (s32[384,8]{0,1:T(8,128)S(1)}, s32[384,8]{0,1:T(8,128)}, u32[]{:S(2)}) copy-start(s32[384,8]{0,1:T(8,128)} %param.9) | copy-start | bytes 36868
  1.3 0.7 %copy-start.1 = (s32[384]{0:T(512)S(1)}, s32[384]{0:T(512)}, u32[]{:S(2)}) copy-start(s32[384]{0:T(512)} %param.8) | copy-start | bytes 4612

commit v2 on v1

--- a/solution.py
+++ b/solution.py
@@ -15,7 +15,6 @@
 PACKED = 45
 ROWS = 56
 NIMG = 16
-NY = 4
 LM_LAMBDA = 0.5
 f32 = jnp.float32
 bf16 = jnp.bfloat16
@@ -30,25 +29,27 @@
 
 
 def marginalize_kernel(
-    jc, jp, rs, cnt, cam, rec_out, coup_out, small_out, cam_out,
-    jcv, jpv, rsv, qt, ta, tb, acc, rec, sem,
+    jc, jp, rs, cnt_hbm, cam_hbm, rec_out, coup_out, small_out, cam_out,
+    jcv, jpv, rsv, qt, ta, tb, acc, rec, cnt, cam, sem,
 ):
     def copy(b, which):
         s = pl.ds(b * 128, 128)
         src, dst = ((jp, jpv), (jc, jcv), (rs, rsv))[which]
         return pltpu.make_async_copy(src.at[s], dst.at[s], sem.at[b, which])
 
+    count_copy = pltpu.make_async_copy(cnt_hbm, cnt, sem.at[NB, 0])
+    cam_copy = pltpu.make_async_copy(cam_hbm, cam, sem.at[NB, 1])
+    count_copy.start()
     for which in range(3):
         for b in range(NB):
             copy(b, which).start()
+        if which == 0:
+            cam_copy.start()
+    count_copy.wait()
 
     jcf = jcv.reshape(NL * CP * K, 128)
     jpf = jpv.reshape(NL * 3 * K, 128)
     rsf = rsv.reshape(NL * K, 128)
-
-    for b in range(NB):
-        for k in range(K):
-            cam_out[0:1, (b * K + k) * 128 : (b * K + k + 1) * 128] = cam[k : k + 1, b * 128 : (b + 1) * 128]
 
     def point_phase(b, _):
         copy(b, 0).wait()
@@ -190,6 +191,10 @@
         return 0
 
     lax.fori_loop(0, NB, camera_phase, 0)
+    cam_copy.wait()
+    for b in range(NB):
+        for k in range(K):
+            cam_out[0:1, (b * K + k) * 128 : (b * K + k + 1) * 128] = cam[k : k + 1, b * 128 : (b + 1) * 128]
 
 
 def marginalize(jac_cam, jac_point, residual, count, cam):
@@ -203,7 +208,7 @@
             jax.ShapeDtypeStruct((NB, 16, 128), f32),
             jax.ShapeDtypeStruct((1, NOBS), jnp.int32),
         ),
-        in_specs=[hbm, hbm, hbm, vmem, vmem],
+        in_specs=[hbm] * 5,
         out_specs=(vmem,) * 4,
         scratch_shapes=[
             pltpu.VMEM((NL, CP, K, 128), f32),
@@ -214,7 +219,9 @@
             pltpu.VMEM((10, 128, 128), f32),
             pltpu.VMEM((len(PAIRS), 64, 128), f32),
             pltpu.VMEM((ROWS * 8, 128), f32),
-            pltpu.SemaphoreType.DMA((NB, 3)),
+            pltpu.VMEM((NB, 128), jnp.int32),
+            pltpu.VMEM((K, NL), jnp.int32),
+            pltpu.SemaphoreType.DMA((NB + 1, 3)),
         ],
         compiler_params=pltpu.CompilerParams(vmem_limit_bytes=52 << 20),
         cost_estimate=pl.CostEstimate(flops=70_000_000, bytes_accessed=21_000_000, transcendentals=0),
@@ -267,19 +274,33 @@
         onehot[:, t * 256 : (t + 1) * 256] = hit.astype(f32).astype(bf16)
 
 
+PLANE = sorted(((a, b) for a in range(4) for b in range(4)), key=lambda q: -min(q[0], 4 - q[0]) - min(q[1], 4 - q[1]))
+OWNERS = 14
+
+
 def camera_kernel(
-    rec, cam, fac_out, steps,
-    onehot, lhs, away, home, from_core, from_y, block, from_img, full, spread,
-    send_a, recv_a, send_b, recv_b, send_c, recv_c, send_d, recv_d, send_e, recv_e,
+    rec, cam, fac_out, steps, pick,
+    onehot, lhs, away, home, from_core, arrived, full, spread,
+    send_a, recv_a, send_c, recv_c, send_d, recv_d, send_e, recv_e,
 ):
     img, mine = lax.axis_index("img"), lax.axis_index("cam")
-    y, core = mine // 2, mine % 2
+    z, x, y, core = img // 4, img % 4, mine // 2, mine % 2
+
+    def plane(q):
+        return ((z + q[0]) % 4) * 4 + (x + q[1]) % 4
 
     barrier = pltpu.get_barrier_semaphore()
-    for d in range(1, NIMG):
-        pl.semaphore_signal(barrier, inc=1, device_id=((img + d) % NIMG, mine), device_id_type=MESH)
-    for d in range(1, 8):
-        pl.semaphore_signal(barrier, inc=1, device_id=(img, (mine + d) % 8), device_id_type=MESH)
+    pl.semaphore_signal(barrier, inc=1, device_id=(img, y * 2 + 1 - core), device_id_type=MESH)
+    for dy in range(4):
+        for q in PLANE:
+            if dy or q != (0, 0):
+                pl.semaphore_signal(
+                    barrier, inc=1, device_id=(plane(q), ((y + dy) % 4) * 2 + core), device_id_type=MESH
+                )
+    for dy in range(1, 4):
+        pl.semaphore_signal(
+            barrier, inc=1, device_id=(img, ((y + dy) % 4) * 2 + 1 - core), device_id_type=MESH
+        )
 
     fill_onehot(cam, onehot)
 
@@ -296,95 +317,96 @@
         )
         return [r[112 * h : 112 * h + 56] + r[112 * h + 56 : 112 * h + 112] for h in range(2)]
 
-    to_core = []
-    for d in range(4):
-        to_y = (y + 2 - d + 4) % 4
-        sums = sums_of(to_y * 2 + 1 - core)
-        for h in range(2):
-            away[d, h] = sums[h]
-        if d == 0:
-            pl.semaphore_wait(barrier, 22)
-        copy = pltpu.make_async_remote_copy(
-            src_ref=away.at[d], dst_ref=from_core.at[d], send_sem=send_a.at[d], recv_sem=recv_a.at[d],
+    ORDER = (2, 1, 3, 0)
+
+    def core_copy(d):
+        return pltpu.make_async_remote_copy(
+            src_ref=away.at[d, pl.ds(0, OWNERS)], dst_ref=from_core.at[d, pl.ds(0, OWNERS)],
+            send_sem=send_a.at[d], recv_sem=recv_a.at[d],
             device_id=(img, y * 2 + 1 - core), device_id_type=MESH,
         )
-        copy.start()
-        to_core.append(copy)
-
-    to_ys = []
-    for d in range(4):
-        away_by = (2 - d + 4) % 4
-        to_y = (y + away_by) % 4
-        sums = sums_of(to_y * 2 + core)
-        to_core[d].wait_recv()
+
+    def other_core(d):
+        sums = sums_of(((y + ORDER[d]) % 4) * 2 + 1 - core)
         for h in range(2):
-            home[d, h] = sums[h] + from_core[d, h]
-        if away_by:
-            copy = pltpu.make_async_remote_copy(
-                src_ref=home.at[d], dst_ref=from_y.at[away_by - 1],
-                send_sem=send_b.at[away_by - 1], recv_sem=recv_b.at[away_by - 1],
-                device_id=(img, to_y * 2 + core), device_id_type=MESH,
-            )
-            copy.start()
-            to_ys.append(copy)
-    own = 2
-    for copy in to_ys:
-        copy.wait_recv()
-    for h in range(2):
-        total = home[own, h] + from_y[0, h] + from_y[1, h] + from_y[2, h]
-        for r in range(7):
-            block[h * 7 + r] = total[8 * r : 8 * r + 8]
-
-    def slice_copy(d):
+            for r in range(7):
+                away[d, h * 7 + r] = sums[h][8 * r : 8 * r + 8]
+        if d == 0:
+            pl.semaphore_wait(barrier, 67)
+        core_copy(d).start()
+
+    def slice_copy(d, q):
+        n = ORDER[d] * 16 + q[0] * 4 + q[1]
         return pltpu.make_async_remote_copy(
-            src_ref=block.at[(img + d) % NIMG], dst_ref=from_img.at[d],
-            send_sem=send_c.at[d], recv_sem=recv_c.at[d],
-            device_id=((img + d) % NIMG, mine), device_id_type=MESH,
+            src_ref=home.at[d, plane(q)], dst_ref=arrived.at[n],
+            send_sem=send_c.at[n], recv_sem=recv_c.at[n],
+            device_id=(plane(q), ((y + ORDER[d]) % 4) * 2 + core), device_id_type=MESH,
         )
 
-    for d in range(1, NIMG):
-        @pl.when((img + d) % NIMG < 14)
-        def _(d=d):
-            slice_copy(d).start()
-
-    def sum_copy(d):
+    def own_core(d):
+        sums = sums_of(((y + ORDER[d]) % 4) * 2 + core)
+        core_copy(d).wait_recv()
+        for h in range(2):
+            for r in range(7):
+                home[d, h * 7 + r] = sums[h][8 * r : 8 * r + 8] + from_core[d, h * 7 + r]
+        for q in PLANE:
+            if ORDER[d] or q != (0, 0):
+                @pl.when(plane(q) < OWNERS)
+                def _(q=q):
+                    slice_copy(d, q).start()
+
+    other_core(0)
+    other_core(1)
+    own_core(0)
+    other_core(2)
+    own_core(1)
+    other_core(3)
+    own_core(2)
+    own_core(3)
+
+    def sum_copy(q):
+        n = q[0] * 4 + q[1]
         return pltpu.make_async_remote_copy(
             src_ref=full.at[img], dst_ref=full.at[img],
-            send_sem=send_d.at[d], recv_sem=recv_d.at[d],
-            device_id=((img + d) % NIMG, mine), device_id_type=MESH,
+            send_sem=send_d.at[n], recv_sem=recv_d.at[n],
+            device_id=(plane(q), mine), device_id_type=MESH,
         )
 
-    @pl.when(img < 14)
+    @pl.when(img < OWNERS)
     def _():
-        for d in range(1, NIMG):
-            slice_copy(d).wait_recv()
-        total = block[img]
-        for d in range(1, NIMG):
-            total = total + from_img[d]
+        total = home[3, img]
+        for d in range(4):
+            for q in PLANE:
+                if ORDER[d] or q != (0, 0):
+                    slice_copy(d, q).wait_recv()
+                    total = total + arrived[ORDER[d] * 16 + q[0] * 4 + q[1]]
         full[img] = total
-        for d in range(1, NIMG):
-            sum_copy(d).start()
-
-    for d in range(1, NIMG):
-        @pl.when((img - d + NIMG) % NIMG < 14)
-        def _(d=d):
-            sum_copy(d).wait_recv()
+        for q in PLANE[:15]:
+            sum_copy(q).start()
+
+    for t in range(NOBS // 256):
+        cols = slice(t * 256, (t + 1) * 256)
+        hit = lax.broadcasted_iota(jnp.int32, (128, 256), 0) == (cam[0:1, cols] & 127)
+        hit = hit.astype(f32).astype(bf16)
+        pick[0:128, cols] = hit
+        pick[128:256, cols] = hit
+
+    for q in PLANE[:15]:
+        @pl.when(plane(((4 - q[0]) % 4, (4 - q[1]) % 4)) < OWNERS)
+        def _(q=q):
+            sum_copy(q).wait_recv()
 
     for h in range(2):
         for r in range(7):
             for e in range(2):
                 spread[pl.ds(r * 32 + h * 2 + e, 8, stride=4), :] = full[h * 7 + r, :, e * 128 : (e + 1) * 128]
     factor, step = camera_solve(lambda c: spread[4 * c : 4 * c + 4, :])
-    for n, v in enumerate(factor):
-        for q in range(4):
-            fac_out[n : n + 1, q * 128 : (q + 1) * 128] = v[q : q + 1]
-    steps[mine] = jnp.zeros((2, 16, 256), f32)
     for n, v in enumerate(step):
-        for q in range(4):
-            steps[mine, q // 2, n : n + 1, (q % 2) * 128 : (q % 2 + 1) * 128] = v[q : q + 1]
+        steps[mine, 4 * n : 4 * n + 4, :] = v
+    steps[mine, 36:40, :] = jnp.zeros((4, 128), f32)
 
     to_cams = []
-    for d in range(1, 8):
+    for d in (4, 5, 3, 2, 6, 7, 1):
         copy = pltpu.make_async_remote_copy(
             src_ref=steps.at[mine], dst_ref=steps.at[mine],
             send_sem=send_e.at[d], recv_sem=recv_e.at[d],
@@ -393,17 +415,22 @@
         copy.start()
         to_cams.append(copy)
 
-    for copy in to_core + to_ys:
-        copy.wait_send()
-    for d in range(1, NIMG):
-        @pl.when((img + d) % NIMG < 14)
-        def _(d=d):
-            slice_copy(d).wait_send()
-
-    @pl.when(img < 14)
+    for n, v in enumerate(factor):
+        for q in range(4):
+            fac_out[n : n + 1, q * 128 : (q + 1) * 128] = v[q : q + 1]
+
+    for d in range(4):
+        core_copy(d).wait_send()
+        for q in PLANE:
+            if ORDER[d] or q != (0, 0):
+                @pl.when(plane(q) < OWNERS)
+                def _(d=d, q=q):
+                    slice_copy(d, q).wait_send()
+
+    @pl.when(img < OWNERS)
     def _():
-        for d in range(1, NIMG):
-            sum_copy(d).wait_send()
+        for q in PLANE[:15]:
+            sum_copy(q).wait_send()
 
     for copy in to_cams:
         copy.wait_recv()
@@ -418,23 +445,21 @@
         camera_kernel,
         out_shape=(
             jax.ShapeDtypeStruct((PACKED, 512), f32),
-            jax.ShapeDtypeStruct((8, 2, 16, 256), f32),
+            jax.ShapeDtypeStruct((8, 40, 128), f32),
+            jax.ShapeDtypeStruct((256, NOBS), bf16),
         ),
         in_specs=[vmem, vmem],
-        out_specs=(vmem, vmem),
+        out_specs=(vmem,) * 3,
         scratch_shapes=[
             pltpu.VMEM((256, NOBS), bf16),
             pltpu.VMEM((224, NOBS), bf16),
-            pltpu.VMEM((4, 2, ROWS, 256), f32),
-            pltpu.VMEM((4, 2, ROWS, 256), f32),
-            pltpu.VMEM((4, 2, ROWS, 256), f32),
-            pltpu.VMEM((3, 2, ROWS, 256), f32),
-            pltpu.VMEM((NIMG, 8, 256), f32),
-            pltpu.VMEM((NIMG, 8, 256), f32),
+            pltpu.VMEM((4, 16, 8, 256), f32),
+            pltpu.VMEM((4, 16, 8, 256), f32),
+            pltpu.VMEM((4, 16, 8, 256), f32),
+            pltpu.VMEM((64, 8, 256), f32),
             pltpu.VMEM((NIMG, 8, 256), f32),
             pltpu.VMEM((ROWS * 4, 128), f32),
-            dma((4,)), dma((4,)), dma((3,)), dma((3,)), dma((NIMG,)), dma((NIMG,)),
-            dma((NIMG,)), dma((NIMG,)), dma((8,)), dma((8,)),
+            dma((4,)), dma((4,)), dma((64,)), dma((64,)), dma((NIMG,)), dma((NIMG,)), dma((8,)), dma((8,)),
         ],
         compiler_params=pltpu.CompilerParams(
             collective_id=0, has_side_effects=True, vmem_limit_bytes=40 << 20
@@ -443,27 +468,31 @@
     )(records, cam)
 
 
-def point_kernel(fac, steps, cam, coup, small, fac_out, step_out, point_out, onehot, picked):
+def point_kernel(fac, steps, pick, cam, coup, small, fac_out, step_out, point_out, picked, groups):
     mine = lax.axis_index("cam")
     fac_out[...] = fac[...]
-    for h in range(2):
-        step_out[:, h * 256 : (h + 1) * 256] = steps[mine, h, 0:CP, :]
-    fill_onehot(cam, onehot)
-    table = steps[...].reshape(256, 256)
-    high = table.astype(bf16)
-    low = (table - high.astype(f32)).astype(bf16)
+    for c in range(CP):
+        for q in range(4):
+            step_out[c : c + 1, q * 128 : (q + 1) * 128] = steps[mine, 4 * c + q : 4 * c + q + 1, :]
+    table = steps[...].reshape(320, 128)
+    high = table.astype(bf16).astype(f32)
+    table = jnp.concatenate([high, table - high], axis=1).astype(bf16)
+    quarter = lax.broadcasted_iota(jnp.int32, (40, 256), 0) & 3
     for b in range(NB):
         for q in range(4):
             cols = slice(b * 1024 + q * 256, b * 1024 + (q + 1) * 256)
-            chosen = jnp.dot(high, onehot[:, cols], preferred_element_type=f32) + jnp.dot(
-                low, onehot[:, cols], preferred_element_type=f32
-            )
-            group = cam[0:1, cols] >> 8
-            total = jnp.zeros((16, 256), f32)
-            for g in range(16):
-                total = total + jnp.where(group == g, chosen[16 * g : 16 * g + 16], 0.0)
+            chosen = jnp.dot(table, pick[:, cols], preferred_element_type=f32)
+            place = (cam[0:1, cols] >> 7) - quarter
+            total = jnp.zeros((40, 256), f32)
+            for g in range(8):
+                total = total + jnp.where(place == 4 * g, chosen[40 * g : 40 * g + 40], 0.0)
             for e in range(2):
-                picked[pl.ds(q * 2 + e, 16, stride=8), :] = total[:, e * 128 : (e + 1) * 128]
+                groups[q * 2 + e] = total[:, e * 128 : (e + 1) * 128]
+        for k in range(K):
+            total = groups[k, pl.ds(0, 10, stride=4), :]
+            for q in range(1, 4):
+                total = total + groups[k, pl.ds(q, 10, stride=4), :]
+            picked[pl.ds(k, 10, stride=8), :] = total
         sums = []
         for p in range(3):
             v = coup[b, p * CP] * picked[0:8, :]
@@ -479,7 +508,7 @@
             point_out[p : p + 1, b * 128 : (b + 1) * 128] = -v
 
 
-def point_update(fac, steps, cam, coup, small):
+def point_update(fac, steps, pick, cam, coup, small):
     vmem = pl.BlockSpec(memory_space=pltpu.MemorySpace.VMEM)
     return pl.pallas_call(
         point_kernel,
@@ -488,12 +517,12 @@
             jax.ShapeDtypeStruct((CP, 512), f32),
             jax.ShapeDtypeStruct((3, NL), f32),
         ),
-        in_specs=[vmem] * 5,
+        in_specs=[vmem] * 6,
         out_specs=(vmem,) * 3,
-        scratch_shapes=[pltpu.VMEM((256, NOBS), bf16), pltpu.VMEM((128, 128), f32)],
+        scratch_shapes=[pltpu.VMEM((80, 128), f32), pltpu.VMEM((K, 40, 128), f32)],
         compiler_params=pltpu.CompilerParams(vmem_limit_bytes=32 << 20),
         name="point_update",
-    )(fac, steps, cam, coup, small)
+    )(fac, steps, pick, cam, coup, small)
 
 
 def local(jac_cam, jac_point, residual, obs_count, obs_camera):
@@ -504,8 +533,8 @@
         obs_count.reshape(NB, 128),
         jnp.transpose(obs_camera),
     )
-    fac, steps = camera_update(records, cam)
-    return point_update(fac, steps, cam, coup, small)
+    fac, steps, pick = camera_update(records, cam)
+    return point_update(fac, steps, pick, cam, coup, small)
 
 
 def solution(mesh):

time: 59.1 us -> 55.6 us (0.941)
  Pallas kernels: 56.8 us -> 53.4 us
    pallas_call x1, Pallas kernels: 35.4 us -> 32.6 us  [camera_update(): pl.pallas_call(camera_kernel, out_shape=(jax.ShapeDtypeStruct((PACKED, 51...]
    pallas_call x1, Pallas kernels: 2.04 us -> 1.35 us  [point_update(): pl.pallas_call(point_kernel, out_shape=(jax.ShapeDtypeStruct((PACKED, 512...]
where the time goes in v2:
time: 55.6 us; the launch traced here: 55.4 us
  Pallas kernels  53.4 us (96%)
  local copies, waits for them, and re-layouts  1.38 us (2%)
  between operations  0.66 us (1%)
    pallas_call x1, Pallas kernels, camera_update(): pl.pallas_call(camera_kernel, out_shape=(jax.ShapeDtypeStruct((PACKED, 51...  32.6 us
    pallas_call x1, Pallas kernels, marginalize(): pl.pallas_call(marginalize_kernel, out_shape=(jax.ShapeDtypeStruct((2 * R...  19.5 us
    unnamed x4, local copies, waits for them, and re-layouts  1.38 us
    pallas_call x1, Pallas kernels, point_update(): pl.pallas_call(point_kernel, out_shape=(jax.ShapeDtypeStruct((PACKED, 512...  1.35 us

profile of v2, /device:TPU:1, one launch (start us, length us, event | category | flops | bytes accessed | tf_op | source)
XLA Modules:
  0.0 55.4 jit_solution(4535863048760422921)
XLA Ops:
  0.6 0.0 copy-start
  0.6 0.7 %copy-done = s32[384,8]{0,1:T(8,128)S(1)} copy-done((s32[384,8]{0,1:T(8,128)S(1)}, s32[384,8]{0,1:T(8,128)}, u32[]{:S(2)}) %copy-start) | copy-done | bytes 12312
  1.3 0.0 copy-start.1
  1.3 0.7 %copy-done.1 = s32[384]{0:T(512)S(1)} copy-done((s32[384]{0:T(512)S(1)}, s32[384]{0:T(512)}, u32[]{:S(2)}) %copy-start.1) | copy-done | bytes 1560
  2.0 19.5 %marginalize.1 = (bf16[112,3072]{1,0:T(8,128)(2,1)S(1)}, f32[3,27,8,128]{3,2,1,0:T(8,128)S(1)}, f32[3,16,128]{2,1,0:T(8,128)S(1)}, s32[1,3072]{1,0:T(1,128)S(1)}) custom-call(f32[384,9,8,128]{3,2,1,0:T(8,128)} %bitcast.6, f32[384,3,8,128]{3,2,1,0:T(8,128)} %bitcast.7, f32[384,8,128]{2,1,0:T(8,128)} %rs.1, s32[3,128]{1,0:T(4,128)S(1)} %bitcast.5, ...), custom_call_target="tpu_custom_call" | custom-call | flops 70000000 | bytes 21000000 | tf_op jit(solution)/shard_map/marginalize/pallas_call | solution.py:203
  21.5 32.6 %camera_update.1 = (f32[45,512]{1,0:T(8,128)S(1)}, f32[8,40,128]{2,1,0:T(8,128)S(1)}, bf16[256,3072]{1,0:T(8,128)(2,1)S(1)}) custom-call(bf16[112,3072]{1,0:T(8,128)(2,1)S(1)} %get-tuple-element.10.rec, s32[1,3072]{1,0:T(1,128)S(1)} %get-tuple-element.11.cam), custom_call_target="tpu_custom_call" | custom-call | tf_op jit(solution)/shard_map/camera_update/pallas_call | solution.py:444
  54.1 1.4 %point_update.1 = (f32[45,512]{1,0:T(8,128)}, f32[9,512]{1,0:T(8,128)}, f32[3,384]{1,0:T(4,128)}) custom-call(f32[45,512]{1,0:T(8,128)S(1)} %get-tuple-element.12.fac, f32[8,40,128]{2,1,0:T(8,128)S(1)} %get-tuple-element.13.steps, bf16[256,3072]{1,0:T(8,128)(2,1)S(1)} %get-tuple-element.14.pick, s32[1,3072]{1,0:T(1,128)S(1)} %get-tuple-element.11.cam, ...), custom_call_target="tpu_custom_call" | custom-call | tf_op jit(solution)/shard_map/point_update/pallas_call | solution.py:513
Async XLA Ops:
  0.6 0.7 %copy-start = (s32[384,8]{0,1:T(8,128)S(1)}, s32[384,8]{0,1:T(8,128)}, u32[]{:S(2)}) copy-start(s32[384,8]{0,1:T(8,128)} %param.9) | copy-start | bytes 36868
  1.3 0.7 %copy-start.1 = (s32[384]{0:T(512)S(1)}, s32[384]{0:T(512)}, u32[]{:S(2)}) copy-start(s32[384]{0:T(512)} %param.8) | copy-start | bytes 4612

commit v3 on v2

--- a/solution.py
+++ b/solution.py
@@ -29,8 +29,8 @@
 
 
 def marginalize_kernel(
-    jc, jp, rs, cnt_hbm, cam_hbm, rec_out, coup_out, small_out, cam_out,
-    jcv, jpv, rsv, qt, ta, tb, acc, rec, cnt, cam, sem,
+    jc, jp, rs, cnt_hbm, cam_hbm, ent_out, small_out, live_out, cam_out,
+    jcv, jpv, rsv, qt, ta, tb, acc, cnt, cam, sem,
 ):
     def copy(b, which):
         s = pl.ds(b * 128, 128)
@@ -155,39 +155,13 @@
 
         lax.fori_loop(0, K // 2, two, 0)
 
-        def entry(n):
+        slot = lax.broadcasted_iota(jnp.int32, (8, 128), 0)
+        live_out[b] = (slot < cnt[pl.ds(b, 1), :]).astype(f32)
+        for n in range(len(PAIRS)):
             v = acc[n, pl.ds(0, 8, stride=8), :]
             for s in range(1, 8):
                 v = v + acc[n, pl.ds(s, 8, stride=8), :]
-            return v
-
-        slot = lax.broadcasted_iota(jnp.int32, (8, 128), 0)
-        live = (slot < cnt[pl.ds(b, 1), :]).astype(f32)
-        inv = [small_out[b, p : p + 1, :] for p in range(3)]
-        coupling = [[entry(54 + p * CP + c) * inv[p] for c in range(CP)] for p in range(3)]
-        for p in range(3):
-            for c in range(CP):
-                coup_out[b, p * CP + c] = coupling[p][c]
-        rhs = [jnp.sum(entry(81 + p), axis=0, keepdims=True) * inv[p] for p in range(3)]
-        for p in range(3):
-            small_out[b, 6 + p : 7 + p, :] = rhs[p]
-        for n, (i, j) in enumerate(CC):
-            v = entry(n) * live
-            for p in range(3):
-                v = v - coupling[p][i] * coupling[p][j]
-            rec[n * 8 : n * 8 + 8, :] = v
-        for i in range(CP):
-            v = entry(45 + i) * live
-            for p in range(3):
-                v = v - coupling[p][i] * rhs[p]
-            rec[(45 + i) * 8 : (45 + i) * 8 + 8, :] = v
-        for i in range(54, ROWS):
-            rec[i * 8 : i * 8 + 8, :] = jnp.zeros((8, 128), f32)
-        for k in range(K):
-            v = rec[pl.ds(k, ROWS, stride=8), :]
-            high = v.astype(bf16).astype(f32)
-            both = jnp.concatenate([high, v - high], axis=0).astype(bf16)
-            rec_out[:, pl.ds(pl.multiple_of((b * K + k) * 128, 128), 128)] = both
+            ent_out[b, n] = v
         return 0
 
     lax.fori_loop(0, NB, camera_phase, 0)
@@ -203,9 +177,9 @@
     return pl.pallas_call(
         marginalize_kernel,
         out_shape=(
-            jax.ShapeDtypeStruct((2 * ROWS, NOBS), bf16),
-            jax.ShapeDtypeStruct((NB, 27, 8, 128), f32),
+            jax.ShapeDtypeStruct((NB, len(PAIRS), 8, 128), f32),
             jax.ShapeDtypeStruct((NB, 16, 128), f32),
+            jax.ShapeDtypeStruct((NB, 8, 128), f32),
             jax.ShapeDtypeStruct((1, NOBS), jnp.int32),
         ),
         in_specs=[hbm] * 5,
@@ -218,7 +192,6 @@
             pltpu.VMEM((10, 128, 128), f32),
             pltpu.VMEM((10, 128, 128), f32),
             pltpu.VMEM((len(PAIRS), 64, 128), f32),
-            pltpu.VMEM((ROWS * 8, 128), f32),
             pltpu.VMEM((NB, 128), jnp.int32),
             pltpu.VMEM((K, NL), jnp.int32),
             pltpu.SemaphoreType.DMA((NB + 1, 3)),
@@ -279,8 +252,8 @@
 
 
 def camera_kernel(
-    rec, cam, fac_out, steps, pick,
-    onehot, lhs, away, home, from_core, arrived, full, spread,
+    ent, small, alive, cam, fac_out, steps, pick, coup_out, rhs_out,
+    rec, turned, onehot, lhs, away, home, from_core, arrived, full, spread,
     send_a, recv_a, send_c, recv_c, send_d, recv_d, send_e, recv_e,
 ):
     img, mine = lax.axis_index("img"), lax.axis_index("cam")
@@ -302,6 +275,39 @@
             barrier, inc=1, device_id=(img, ((y + dy) % 4) * 2 + 1 - core), device_id_type=MESH
         )
 
+    def entry(b, n):
+        return ent[b, n]
+
+    def records(b, _):
+        live = alive[b]
+        inv = [small[b, p : p + 1, :] for p in range(3)]
+        coupling = [[entry(b, 54 + p * CP + c) * inv[p] for c in range(CP)] for p in range(3)]
+        for p in range(3):
+            for c in range(CP):
+                coup_out[b, p * CP + c] = coupling[p][c]
+        rhs = [jnp.sum(entry(b, 81 + p), axis=0, keepdims=True) * inv[p] for p in range(3)]
+        for p in range(3):
+            rhs_out[b, p : p + 1, :] = rhs[p]
+        for n, (i, j) in enumerate(CC):
+            v = entry(b, n) * live
+            for p in range(3):
+                v = v - coupling[p][i] * coupling[p][j]
+            turned[n * 8 : n * 8 + 8, :] = v
+        for i in range(CP):
+            v = entry(b, 45 + i) * live
+            for p in range(3):
+                v = v - coupling[p][i] * rhs[p]
+            turned[(45 + i) * 8 : (45 + i) * 8 + 8, :] = v
+        for i in range(54, ROWS):
+            turned[i * 8 : i * 8 + 8, :] = jnp.zeros((8, 128), f32)
+        for k in range(K):
+            v = turned[pl.ds(k, ROWS, stride=8), :]
+            high = v.astype(bf16).astype(f32)
+            both = jnp.concatenate([high, v - high], axis=0).astype(bf16)
+            rec[:, pl.ds(pl.multiple_of((b * K + k) * 128, 128), 128)] = both
+        return 0
+
+    lax.fori_loop(0, NB, records, 0)
     fill_onehot(cam, onehot)
 
     def sums_of(owner):
@@ -331,9 +337,6 @@
         for h in range(2):
             for r in range(7):
                 away[d, h * 7 + r] = sums[h][8 * r : 8 * r + 8]
-        if d == 0:
-            pl.semaphore_wait(barrier, 67)
-        core_copy(d).start()
 
     def slice_copy(d, q):
         n = ORDER[d] * 16 + q[0] * 4 + q[1]
@@ -355,14 +358,13 @@
                 def _(q=q):
                     slice_copy(d, q).start()
 
-    other_core(0)
-    other_core(1)
-    own_core(0)
-    other_core(2)
-    own_core(1)
-    other_core(3)
-    own_core(2)
-    own_core(3)
+    for d in range(4):
+        other_core(d)
+    pl.semaphore_wait(barrier, 67)
+    for d in range(4):
+        core_copy(d).start()
+    for d in range(4):
+        own_core(d)
 
     def sum_copy(q):
         n = q[0] * 4 + q[1]
@@ -438,7 +440,7 @@
         copy.wait_send()
 
 
-def camera_update(records, cam):
+def camera_update(ent, small, alive, cam):
     vmem = pl.BlockSpec(memory_space=pltpu.MemorySpace.VMEM)
     dma = pltpu.SemaphoreType.DMA
     return pl.pallas_call(
@@ -447,10 +449,14 @@
             jax.ShapeDtypeStruct((PACKED, 512), f32),
             jax.ShapeDtypeStruct((8, 40, 128), f32),
             jax.ShapeDtypeStruct((256, NOBS), bf16),
+            jax.ShapeDtypeStruct((NB, 27, 8, 128), f32),
+            jax.ShapeDtypeStruct((NB, 8, 128), f32),
         ),
-        in_specs=[vmem, vmem],
-        out_specs=(vmem,) * 3,
+        in_specs=[vmem] * 4,
+        out_specs=(vmem,) * 5,
         scratch_shapes=[
+            pltpu.VMEM((2 * ROWS, NOBS), bf16),
+            pltpu.VMEM((ROWS * 8, 128), f32),
             pltpu.VMEM((256, NOBS), bf16),
             pltpu.VMEM((224, NOBS), bf16),
             pltpu.VMEM((4, 16, 8, 256), f32),
@@ -465,10 +471,10 @@
             collective_id=0, has_side_effects=True, vmem_limit_bytes=40 << 20
         ),
         name="camera_update",
-    )(records, cam)
-
-
-def point_kernel(fac, steps, pick, cam, coup, small, fac_out, step_out, point_out, picked, groups):
+    )(ent, small, alive, cam)
+
+
+def point_kernel(fac, steps, pick, cam, coup, small, rhs, fac_out, step_out, point_out, picked, groups):
     mine = lax.axis_index("cam")
     fac_out[...] = fac[...]
     for c in range(CP):
@@ -498,7 +504,7 @@
             v = coup[b, p * CP] * picked[0:8, :]
             for c in range(1, CP):
                 v = v + coup[b, p * CP + c] * picked[c * 8 : c * 8 + 8, :]
-            sums.append(small[b, 6 + p : 7 + p, :] + jnp.sum(v, axis=0, keepdims=True))
+            sums.append(rhs[b, p : p + 1, :] + jnp.sum(v, axis=0, keepdims=True))
         inv = [small[b, p : p + 1, :] for p in range(3)]
         r01, r02, r12 = [small[b, p : p + 1, :] for p in range(3, 6)]
         two = sums[2] * inv[2]
@@ -508,7 +514,7 @@
             point_out[p : p + 1, b * 128 : (b + 1) * 128] = -v
 
 
-def point_update(fac, steps, pick, cam, coup, small):
+def point_update(fac, steps, pick, cam, coup, small, rhs):
     vmem = pl.BlockSpec(memory_space=pltpu.MemorySpace.VMEM)
     return pl.pallas_call(
         point_kernel,
@@ -517,24 +523,24 @@
             jax.ShapeDtypeStruct((CP, 512), f32),
             jax.ShapeDtypeStruct((3, NL), f32),
         ),
-        in_specs=[vmem] * 6,
+        in_specs=[vmem] * 7,
         out_specs=(vmem,) * 3,
         scratch_shapes=[pltpu.VMEM((80, 128), f32), pltpu.VMEM((K, 40, 128), f32)],
         compiler_params=pltpu.CompilerParams(vmem_limit_bytes=32 << 20),
         name="point_update",
-    )(fac, steps, pick, cam, coup, small)
+    )(fac, steps, pick, cam, coup, small, rhs)
 
 
 def local(jac_cam, jac_point, residual, obs_count, obs_camera):
-    records, coup, small, cam = marginalize(
+    ent, small, alive, cam = marginalize(
         jnp.transpose(jac_cam, (0, 2, 1, 3)),
         jnp.transpose(jac_point, (0, 2, 1, 3)),
         residual,
         obs_count.reshape(NB, 128),
         jnp.transpose(obs_camera),
     )
-    fac, steps, pick = camera_update(records, cam)
-    return point_update(fac, steps, pick, cam, coup, small)
+    fac, steps, pick, coup, rhs = camera_update(ent, small, alive, cam)
+    return point_update(fac, steps, pick, cam, coup, small, rhs)
 
 
 def solution(mesh):

time: 55.6 us -> 54.2 us (0.975)
  Pallas kernels: 53.4 us -> 52 us
    pallas_call x1, Pallas kernels: 32.6 us -> 31.4 us  [camera_update(): pl.pallas_call(camera_kernel, out_shape=(jax.ShapeDtypeStruct((PACKED, 51...]
where the time goes in v3:
time: 54.2 us; the launch traced here: 54 us
  Pallas kernels  52 us (96%)
  local copies, waits for them, and re-layouts  1.38 us (3%)
  between operations  0.66 us (1%)
    pallas_call x1, Pallas kernels, camera_update(): pl.pallas_call(camera_kernel, out_shape=(jax.ShapeDtypeStruct((PACKED, 51...  31.4 us
    pallas_call x1, Pallas kernels, marginalize(): pl.pallas_call(marginalize_kernel, out_shape=(jax.ShapeDtypeStruct((NB, l...  19.2 us
    unnamed x4, local copies, waits for them, and re-layouts  1.38 us
    pallas_call x1, Pallas kernels, point_update(): pl.pallas_call(point_kernel, out_shape=(jax.ShapeDtypeStruct((PACKED, 512...  1.34 us

profile of v3, /device:TPU:1, one launch (start us, length us, event | category | flops | bytes accessed | tf_op | source)
XLA Modules:
  0.0 54.0 jit_solution(2661522225195743223)
XLA Ops:
  0.6 0.0 copy-start
  0.6 0.7 %copy-done = s32[384,8]{0,1:T(8,128)S(1)} copy-done((s32[384,8]{0,1:T(8,128)S(1)}, s32[384,8]{0,1:T(8,128)}, u32[]{:S(2)}) %copy-start) | copy-done | bytes 12312
  1.3 0.0 copy-start.1
  1.3 0.7 %copy-done.1 = s32[384]{0:T(512)S(1)} copy-done((s32[384]{0:T(512)S(1)}, s32[384]{0:T(512)}, u32[]{:S(2)}) %copy-start.1) | copy-done | bytes 1560
  2.0 19.2 %marginalize.1 = (f32[3,84,8,128]{3,2,1,0:T(8,128)S(1)}, f32[3,16,128]{2,1,0:T(8,128)S(1)}, f32[3,8,128]{2,1,0:T(8,128)S(1)}, s32[1,3072]{1,0:T(1,128)S(1)}) custom-call(f32[384,9,8,128]{3,2,1,0:T(8,128)} %bitcast.6, f32[384,3,8,128]{3,2,1,0:T(8,128)} %bitcast.7, f32[384,8,128]{2,1,0:T(8,128)} %rs.1, s32[3,128]{1,0:T(4,128)S(1)} %bitcast.5, s32[8,384]{1,0:T(8,128)S(1)} %bitcast.4), custom_call_target="tpu_custom_call" | custom-call | flops 70000000 | bytes 21000000 | tf_op jit(solution)/shard_map/marginalize/pallas_call | solution.py:177
  21.2 31.4 %camera_update.1 = (f32[45,512]{1,0:T(8,128)S(1)}, f32[8,40,128]{2,1,0:T(8,128)S(1)}, bf16[256,3072]{1,0:T(8,128)(2,1)S(1)}, f32[3,27,8,128]{3,2,1,0:T(8,128)S(1)}, f32[3,8,128]{2,1,0:T(8,128)S(1)}) custom-call(f32[3,84,8,128]{3,2,1,0:T(8,128)S(1)} %get-tuple-element.12.ent, f32[3,16,128]{2,1,0:T(8,128)S(1)} %get-tuple-element.13.small, ...), custom_call_target="tpu_custom_call" | custom-call | tf_op jit(solution)/shard_map/camera_update/pallas_call | solution.py:446
  52.7 1.3 %point_update.1 = (f32[45,512]{1,0:T(8,128)}, f32[9,512]{1,0:T(8,128)}, f32[3,384]{1,0:T(4,128)}) custom-call(f32[45,512]{1,0:T(8,128)S(1)} %get-tuple-element.16.fac, f32[8,40,128]{2,1,0:T(8,128)S(1)} %get-tuple-element.17.steps, bf16[256,3072]{1,0:T(8,128)(2,1)S(1)} %get-tuple-element.18.pick, s32[1,3072]{1,0:T(1,128)S(1)} %get-tuple-element.15.cam, ...), custom_call_target="tpu_custom_call" | custom-call | tf_op jit(solution)/shard_map/point_update/pallas_call | solution.py:519
Async XLA Ops:
  0.6 0.7 %copy-start = (s32[384,8]{0,1:T(8,128)S(1)}, s32[384,8]{0,1:T(8,128)}, u32[]{:S(2)}) copy-start(s32[384,8]{0,1:T(8,128)} %param.9) | copy-start | bytes 36868
  1.3 0.7 %copy-start.1 = (s32[384]{0:T(512)S(1)}, s32[384]{0:T(512)}, u32[]{:S(2)}) copy-start(s32[384]{0:T(512)} %param.8) | copy-start | bytes 4612

commit v4 on v2

--- a/solution.py
+++ b/solution.py
@@ -26,207 +26,6 @@
 QR = [(10 + p, 9) for p in range(3)]
 PAIRS = CC + CR + QC + QR
 GROUPS = [PAIRS[0:28], PAIRS[28:56], PAIRS[56:84]]
-
-
-def marginalize_kernel(
-    jc, jp, rs, cnt_hbm, cam_hbm, rec_out, coup_out, small_out, cam_out,
-    jcv, jpv, rsv, qt, ta, tb, acc, rec, cnt, cam, sem,
-):
-    def copy(b, which):
-        s = pl.ds(b * 128, 128)
-        src, dst = ((jp, jpv), (jc, jcv), (rs, rsv))[which]
-        return pltpu.make_async_copy(src.at[s], dst.at[s], sem.at[b, which])
-
-    count_copy = pltpu.make_async_copy(cnt_hbm, cnt, sem.at[NB, 0])
-    cam_copy = pltpu.make_async_copy(cam_hbm, cam, sem.at[NB, 1])
-    count_copy.start()
-    for which in range(3):
-        for b in range(NB):
-            copy(b, which).start()
-        if which == 0:
-            cam_copy.start()
-    count_copy.wait()
-
-    jcf = jcv.reshape(NL * CP * K, 128)
-    jpf = jpv.reshape(NL * 3 * K, 128)
-    rsf = rsv.reshape(NL * K, 128)
-
-    def point_phase(b, _):
-        copy(b, 0).wait()
-        count = cnt[pl.ds(b, 1), :]
-        zero = jnp.zeros((8, 128), f32)
-
-        def first(k, sums):
-            live = (count > k).astype(f32)
-            parts = []
-            for p in range(3):
-                v = jpf[pl.ds(b * (128 * 3 * K) + p * K + k, 128, stride=3 * K), :].T * live
-                qt[p, b * K + k] = v
-                parts.append(v)
-            sums = list(sums)
-            for x in range(16):
-                a = [v[8 * x : 8 * x + 8] for v in parts]
-                for q in range(3):
-                    sums[q] = sums[q] + a[0] * a[q]
-            return tuple(sums)
-
-        s00, s01, s02 = [
-            jnp.sum(v, axis=0, keepdims=True) for v in lax.fori_loop(0, K, first, (zero,) * 3)
-        ]
-        norm0 = jnp.sqrt(s00)
-        inv0 = 1.0 / norm0
-        r01 = s01 * inv0
-        r02 = s02 * inv0
-        c01 = r01 * inv0
-        c02 = r02 * inv0
-
-        def second(k, sums):
-            n1, s12 = sums
-            for x in range(16):
-                rows = pl.ds(8 * x, 8)
-                rem = qt[1, b * K + k, rows, :] - c01 * qt[0, b * K + k, rows, :]
-                qt[1, b * K + k, rows, :] = rem
-                n1 = n1 + rem * rem
-                s12 = s12 + rem * qt[2, b * K + k, rows, :]
-            return n1, s12
-
-        n11, s12 = [
-            jnp.sum(v, axis=0, keepdims=True) for v in lax.fori_loop(0, K, second, (zero,) * 2)
-        ]
-        norm1 = jnp.sqrt(n11)
-        inv1 = 1.0 / norm1
-        r12 = s12 * inv1
-        c12 = r12 * inv1
-
-        def third(k, n2):
-            for x in range(16):
-                rows = pl.ds(8 * x, 8)
-                rem = (
-                    qt[2, b * K + k, rows, :]
-                    - c02 * qt[0, b * K + k, rows, :]
-                    - c12 * qt[1, b * K + k, rows, :]
-                )
-                qt[2, b * K + k, rows, :] = rem
-                n2 = n2 + rem * rem
-            return n2
-
-        n22 = jnp.sum(lax.fori_loop(0, K, third, zero), axis=0, keepdims=True)
-        norm2 = jnp.sqrt(n22)
-        inv2 = 1.0 / norm2
-        for n, v in enumerate((inv0, inv1, inv2, r01, r02, r12)):
-            small_out[b, n : n + 1, :] = v
-        return 0
-
-    lax.fori_loop(0, NB, point_phase, 0)
-
-    def turn(b, k, t):
-        for c in range(CP):
-            t[c] = jcf[pl.ds(b * (128 * CP * K) + c * K + k, 128, stride=CP * K), :].T
-        t[9] = rsf[pl.ds(b * (128 * K) + k, 128, stride=K), :].T
-
-    def products(b, k, t):
-        base = 0
-        for pairs in GROUPS:
-            total = [None] * len(pairs)
-            for x in range(16):
-                rows = pl.ds(8 * x, 8)
-                held = {}
-                for n, pair in enumerate(pairs):
-                    for q in pair:
-                        if q not in held:
-                            held[q] = t[q, rows, :] if q < 10 else qt[q - 10, b * K + k, rows, :]
-                    term = held[pair[0]] * held[pair[1]]
-                    total[n] = term if total[n] is None else total[n] + term
-            for n in range(len(pairs)):
-                acc[base + n, pl.ds(pl.multiple_of(k * 8, 8), 8), :] = total[n]
-            base += len(pairs)
-
-    def camera_phase(b, _):
-        copy(b, 1).wait()
-        copy(b, 2).wait()
-        turn(b, 0, ta)
-
-        def two(h, _):
-            turn(b, 2 * h + 1, tb)
-            products(b, 2 * h, ta)
-            turn(b, jnp.minimum(2 * h + 2, K - 1), ta)
-            products(b, 2 * h + 1, tb)
-            return 0
-
-        lax.fori_loop(0, K // 2, two, 0)
-
-        def entry(n):
-            v = acc[n, pl.ds(0, 8, stride=8), :]
-            for s in range(1, 8):
-                v = v + acc[n, pl.ds(s, 8, stride=8), :]
-            return v
-
-        slot = lax.broadcasted_iota(jnp.int32, (8, 128), 0)
-        live = (slot < cnt[pl.ds(b, 1), :]).astype(f32)
-        inv = [small_out[b, p : p + 1, :] for p in range(3)]
-        coupling = [[entry(54 + p * CP + c) * inv[p] for c in range(CP)] for p in range(3)]
-        for p in range(3):
-            for c in range(CP):
-                coup_out[b, p * CP + c] = coupling[p][c]
-        rhs = [jnp.sum(entry(81 + p), axis=0, keepdims=True) * inv[p] for p in range(3)]
-        for p in range(3):
-            small_out[b, 6 + p : 7 + p, :] = rhs[p]
-        for n, (i, j) in enumerate(CC):
-            v = entry(n) * live
-            for p in range(3):
-                v = v - coupling[p][i] * coupling[p][j]
-            rec[n * 8 : n * 8 + 8, :] = v
-        for i in range(CP):
-            v = entry(45 + i) * live
-            for p in range(3):
-                v = v - coupling[p][i] * rhs[p]
-            rec[(45 + i) * 8 : (45 + i) * 8 + 8, :] = v
-        for i in range(54, ROWS):
-            rec[i * 8 : i * 8 + 8, :] = jnp.zeros((8, 128), f32)
-        for k in range(K):
-            v = rec[pl.ds(k, ROWS, stride=8), :]
-            high = v.astype(bf16).astype(f32)
-            both = jnp.concatenate([high, v - high], axis=0).astype(bf16)
-            rec_out[:, pl.ds(pl.multiple_of((b * K + k) * 128, 128), 128)] = both
-        return 0
-
-    lax.fori_loop(0, NB, camera_phase, 0)
-    cam_copy.wait()
-    for b in range(NB):
-        for k in range(K):
-            cam_out[0:1, (b * K + k) * 128 : (b * K + k + 1) * 128] = cam[k : k + 1, b * 128 : (b + 1) * 128]
-
-
-def marginalize(jac_cam, jac_point, residual, count, cam):
-    hbm = pl.BlockSpec(memory_space=pltpu.MemorySpace.HBM)
-    vmem = pl.BlockSpec(memory_space=pltpu.MemorySpace.VMEM)
-    return pl.pallas_call(
-        marginalize_kernel,
-        out_shape=(
-            jax.ShapeDtypeStruct((2 * ROWS, NOBS), bf16),
-            jax.ShapeDtypeStruct((NB, 27, 8, 128), f32),
-            jax.ShapeDtypeStruct((NB, 16, 128), f32),
-            jax.ShapeDtypeStruct((1, NOBS), jnp.int32),
-        ),
-        in_specs=[hbm] * 5,
-        out_specs=(vmem,) * 4,
-        scratch_shapes=[
-            pltpu.VMEM((NL, CP, K, 128), f32),
-            pltpu.VMEM((NL, 3, K, 128), f32),
-            pltpu.VMEM((NL, K, 128), f32),
-            pltpu.VMEM((3, NB * K, 128, 128), f32),
-            pltpu.VMEM((10, 128, 128), f32),
-            pltpu.VMEM((10, 128, 128), f32),
-            pltpu.VMEM((len(PAIRS), 64, 128), f32),
-            pltpu.VMEM((ROWS * 8, 128), f32),
-            pltpu.VMEM((NB, 128), jnp.int32),
-            pltpu.VMEM((K, NL), jnp.int32),
-            pltpu.SemaphoreType.DMA((NB + 1, 3)),
-        ],
-        compiler_params=pltpu.CompilerParams(vmem_limit_bytes=52 << 20),
-        cost_estimate=pl.CostEstimate(flops=70_000_000, bytes_accessed=21_000_000, transcendentals=0),
-        name="marginalize",
-    )(jac_cam, jac_point, residual, count, cam)
 
 
 def pair_positions():
@@ -279,8 +78,9 @@
 
 
 def camera_kernel(
-    rec, cam, fac_out, steps, pick,
-    onehot, lhs, away, home, from_core, arrived, full, spread,
+    jc, jp, rs, cnt_hbm, cam_hbm, fac_out, steps, pick, coup_out, small_out, cam_out,
+    jcv, jpv, rsv, qt, ta, tb, acc, cnt, cam, sem,
+    rec, turned, onehot, lhs, away, home, from_core, arrived, full, spread,
     send_a, recv_a, send_c, recv_c, send_d, recv_d, send_e, recv_e,
 ):
     img, mine = lax.axis_index("img"), lax.axis_index("cam")
@@ -302,13 +102,177 @@
             barrier, inc=1, device_id=(img, ((y + dy) % 4) * 2 + 1 - core), device_id_type=MESH
         )
 
-    fill_onehot(cam, onehot)
+    def copy(b, which):
+        s = pl.ds(b * 128, 128)
+        src, dst = ((jp, jpv), (jc, jcv), (rs, rsv))[which]
+        return pltpu.make_async_copy(src.at[s], dst.at[s], sem.at[b, which])
+
+    count_copy = pltpu.make_async_copy(cnt_hbm, cnt, sem.at[NB, 0])
+    cam_copy = pltpu.make_async_copy(cam_hbm, cam, sem.at[NB, 1])
+    count_copy.start()
+    for which in range(3):
+        for b in range(NB):
+            copy(b, which).start()
+        if which == 0:
+            cam_copy.start()
+    count_copy.wait()
+
+    jcf = jcv.reshape(NL * CP * K, 128)
+    jpf = jpv.reshape(NL * 3 * K, 128)
+    rsf = rsv.reshape(NL * K, 128)
+
+    def point_phase(b, _):
+        copy(b, 0).wait()
+        count = cnt[pl.ds(b, 1), :]
+        zero = jnp.zeros((8, 128), f32)
+
+        def first(k, sums):
+            live = (count > k).astype(f32)
+            parts = []
+            for p in range(3):
+                v = jpf[pl.ds(b * (128 * 3 * K) + p * K + k, 128, stride=3 * K), :].T * live
+                qt[p, b * K + k] = v
+                parts.append(v)
+            sums = list(sums)
+            for x in range(16):
+                a = [v[8 * x : 8 * x + 8] for v in parts]
+                for q in range(3):
+                    sums[q] = sums[q] + a[0] * a[q]
+            return tuple(sums)
+
+        s00, s01, s02 = [
+            jnp.sum(v, axis=0, keepdims=True) for v in lax.fori_loop(0, K, first, (zero,) * 3)
+        ]
+        norm0 = jnp.sqrt(s00)
+        inv0 = 1.0 / norm0
+        r01 = s01 * inv0
+        r02 = s02 * inv0
+        c01 = r01 * inv0
+        c02 = r02 * inv0
+
+        def second(k, sums):
+            n1, s12 = sums
+            for x in range(16):
+                rows = pl.ds(8 * x, 8)
+                rem = qt[1, b * K + k, rows, :] - c01 * qt[0, b * K + k, rows, :]
+                qt[1, b * K + k, rows, :] = rem
+                n1 = n1 + rem * rem
+                s12 = s12 + rem * qt[2, b * K + k, rows, :]
+            return n1, s12
+
+        n11, s12 = [
+            jnp.sum(v, axis=0, keepdims=True) for v in lax.fori_loop(0, K, second, (zero,) * 2)
+        ]
+        norm1 = jnp.sqrt(n11)
+        inv1 = 1.0 / norm1
+        r12 = s12 * inv1
+        c12 = r12 * inv1
+
+        def third(k, n2):
+            for x in range(16):
+                rows = pl.ds(8 * x, 8)
+                rem = (
+                    qt[2, b * K + k, rows, :]
+                    - c02 * qt[0, b * K + k, rows, :]
+                    - c12 * qt[1, b * K + k, rows, :]
+                )
+                qt[2, b * K + k, rows, :] = rem
+                n2 = n2 + rem * rem
+            return n2
+
+        n22 = jnp.sum(lax.fori_loop(0, K, third, zero), axis=0, keepdims=True)
+        norm2 = jnp.sqrt(n22)
+        inv2 = 1.0 / norm2
+        for n, v in enumerate((inv0, inv1, inv2, r01, r02, r12)):
+            small_out[b, n : n + 1, :] = v
+        return 0
+
+    lax.fori_loop(0, NB, point_phase, 0)
+
+    def turn(b, k, t):
+        for c in range(CP):
+            t[c] = jcf[pl.ds(b * (128 * CP * K) + c * K + k, 128, stride=CP * K), :].T
+        t[9] = rsf[pl.ds(b * (128 * K) + k, 128, stride=K), :].T
+
+    def products(b, k, t):
+        base = 0
+        for pairs in GROUPS:
+            total = [None] * len(pairs)
+            for x in range(16):
+                rows = pl.ds(8 * x, 8)
+                held = {}
+                for n, pair in enumerate(pairs):
+                    for q in pair:
+                        if q not in held:
+                            held[q] = t[q, rows, :] if q < 10 else qt[q - 10, b * K + k, rows, :]
+                    term = held[pair[0]] * held[pair[1]]
+                    total[n] = term if total[n] is None else total[n] + term
+            for n in range(len(pairs)):
+                acc[base + n, pl.ds(pl.multiple_of(k * 8, 8), 8), :] = total[n]
+            base += len(pairs)
+
+    def camera_phase(b, _):
+        copy(b, 1).wait()
+        copy(b, 2).wait()
+        turn(b, 0, ta)
+
+        def two(h, _):
+            turn(b, 2 * h + 1, tb)
+            products(b, 2 * h, ta)
+            turn(b, jnp.minimum(2 * h + 2, K - 1), ta)
+            products(b, 2 * h + 1, tb)
+            return 0
+
+        lax.fori_loop(0, K // 2, two, 0)
+
+        def entry(n):
+            v = acc[n, pl.ds(0, 8, stride=8), :]
+            for s in range(1, 8):
+                v = v + acc[n, pl.ds(s, 8, stride=8), :]
+            return v
+
+        slot = lax.broadcasted_iota(jnp.int32, (8, 128), 0)
+        live = (slot < cnt[pl.ds(b, 1), :]).astype(f32)
+        inv = [small_out[b, p : p + 1, :] for p in range(3)]
+        coupling = [[entry(54 + p * CP + c) * inv[p] for c in range(CP)] for p in range(3)]
+        for p in range(3):
+            for c in range(CP):
+                coup_out[b, p * CP + c] = coupling[p][c]
+        rhs = [jnp.sum(entry(81 + p), axis=0, keepdims=True) * inv[p] for p in range(3)]
+        for p in range(3):
+            small_out[b, 6 + p : 7 + p, :] = rhs[p]
+        for n, (i, j) in enumerate(CC):
+            v = entry(n) * live
+            for p in range(3):
+                v = v - coupling[p][i] * coupling[p][j]
+            turned[n * 8 : n * 8 + 8, :] = v
+        for i in range(CP):
+            v = entry(45 + i) * live
+            for p in range(3):
+                v = v - coupling[p][i] * rhs[p]
+            turned[(45 + i) * 8 : (45 + i) * 8 + 8, :] = v
+        for i in range(54, ROWS):
+            turned[i * 8 : i * 8 + 8, :] = jnp.zeros((8, 128), f32)
+        for k in range(K):
+            v = turned[pl.ds(k, ROWS, stride=8), :]
+            high = v.astype(bf16).astype(f32)
+            both = jnp.concatenate([high, v - high], axis=0).astype(bf16)
+            rec[:, pl.ds(pl.multiple_of((b * K + k) * 128, 128), 128)] = both
+        return 0
+
+    lax.fori_loop(0, NB, camera_phase, 0)
+    cam_copy.wait()
+    for b in range(NB):
+        for k in range(K):
+            cam_out[0:1, (b * K + k) * 128 : (b * K + k + 1) * 128] = cam[k : k + 1, b * 128 : (b + 1) * 128]
+
+    fill_onehot(cam_out, onehot)
 
     def sums_of(owner):
         for half in range(2):
             for t in range(6):
                 cols = slice(t * 512, (t + 1) * 512)
-                hit = (cam[0:1, cols] >> 8) == owner * 2 + half
+                hit = (cam_out[0:1, cols] >> 8) == owner * 2 + half
                 mask = jnp.broadcast_to(hit.astype(f32), (16, 512)).astype(bf16)
                 mask = jnp.concatenate([mask] * 7, axis=0)
                 lhs[half * 112 : (half + 1) * 112, cols] = rec[:, cols] * mask
@@ -331,8 +295,6 @@
         for h in range(2):
             for r in range(7):
                 away[d, h * 7 + r] = sums[h][8 * r : 8 * r + 8]
-        if d == 0:
-            pl.semaphore_wait(barrier, 67)
         core_copy(d).start()
 
     def slice_copy(d, q):
@@ -355,6 +317,7 @@
                 def _(q=q):
                     slice_copy(d, q).start()
 
+    pl.semaphore_wait(barrier, 67)
     other_core(0)
     other_core(1)
     own_core(0)
@@ -386,7 +349,7 @@
 
     for t in range(NOBS // 256):
         cols = slice(t * 256, (t + 1) * 256)
-        hit = lax.broadcasted_iota(jnp.int32, (128, 256), 0) == (cam[0:1, cols] & 127)
+        hit = lax.broadcasted_iota(jnp.int32, (128, 256), 0) == (cam_out[0:1, cols] & 127)
         hit = hit.astype(f32).astype(bf16)
         pick[0:128, cols] = hit
         pick[128:256, cols] = hit
@@ -438,7 +401,8 @@
         copy.wait_send()
 
 
-def camera_update(records, cam):
+def camera_update(jac_cam, jac_point, residual, count, cam):
+    hbm = pl.BlockSpec(memory_space=pltpu.MemorySpace.HBM)
     vmem = pl.BlockSpec(memory_space=pltpu.MemorySpace.VMEM)
     dma = pltpu.SemaphoreType.DMA
     return pl.pallas_call(
@@ -447,10 +411,25 @@
             jax.ShapeDtypeStruct((PACKED, 512), f32),
             jax.ShapeDtypeStruct((8, 40, 128), f32),
             jax.ShapeDtypeStruct((256, NOBS), bf16),
+            jax.ShapeDtypeStruct((NB, 27, 8, 128), f32),
+            jax.ShapeDtypeStruct((NB, 16, 128), f32),
+            jax.ShapeDtypeStruct((1, NOBS), jnp.int32),
         ),
-        in_specs=[vmem, vmem],
-        out_specs=(vmem,) * 3,
+        in_specs=[hbm] * 5,
+        out_specs=(vmem,) * 6,
         scratch_shapes=[
+            pltpu.VMEM((NL, CP, K, 128), f32),
+            pltpu.VMEM((NL, 3, K, 128), f32),
+            pltpu.VMEM((NL, K, 128), f32),
+            pltpu.VMEM((3, NB * K, 128, 128), f32),
+            pltpu.VMEM((10, 128, 128), f32),
+            pltpu.VMEM((10, 128, 128), f32),
+            pltpu.VMEM((len(PAIRS), 64, 128), f32),
+            pltpu.VMEM((NB, 128), jnp.int32),
+            pltpu.VMEM((K, NL), jnp.int32),
+            pltpu.SemaphoreType.DMA((NB + 1, 3)),
+            pltpu.VMEM((2 * ROWS, NOBS), bf16),
+            pltpu.VMEM((ROWS * 8, 128), f32),
             pltpu.VMEM((256, NOBS), bf16),
             pltpu.VMEM((224, NOBS), bf16),
             pltpu.VMEM((4, 16, 8, 256), f32),
@@ -462,10 +441,10 @@
             dma((4,)), dma((4,)), dma((64,)), dma((64,)), dma((NIMG,)), dma((NIMG,)), dma((8,)), dma((8,)),
         ],
         compiler_params=pltpu.CompilerParams(
-            collective_id=0, has_side_effects=True, vmem_limit_bytes=40 << 20
+            collective_id=0, has_side_effects=True, vmem_limit_bytes=50 << 20
         ),
-        name="camera_update",
-    )(records, cam)
+        name="marginalize_and_sum",
+    )(jac_cam, jac_point, residual, count, cam)
 
 
 def point_kernel(fac, steps, pick, cam, coup, small, fac_out, step_out, point_out, picked, groups):
@@ -526,14 +505,15 @@
 
 
 def local(jac_cam, jac_point, residual, obs_count, obs_camera):
-    records, coup, small, cam = marginalize(
+    operands = (
         jnp.transpose(jac_cam, (0, 2, 1, 3)),
         jnp.transpose(jac_point, (0, 2, 1, 3)),
         residual,
         obs_count.reshape(NB, 128),
         jnp.transpose(obs_camera),
     )
-    fac, steps, pick = camera_update(records, cam)
+    operands = [pltpu.with_memory_space_constraint(v, pltpu.MemorySpace.HBM) for v in operands]
+    fac, steps, pick, coup, small, cam = camera_update(*operands)
     return point_update(fac, steps, pick, cam, coup, small)
 
 

time: 55.6 us -> 51.9 us (0.933)
  Pallas kernels: 53.4 us -> 51.2 us
  local copies, waits for them, and re-layouts: 1.38 us -> 0 us
    pallas_call x1 -> x0, Pallas kernels: 19.5 us -> none  [marginalize(): pl.pallas_call(marginalize_kernel, out_shape=(jax.ShapeDtypeStruct((2 * R...]
    pallas_call x1, Pallas kernels: 32.6 us -> 49.9 us  [camera_update(): pl.pallas_call(camera_kernel, out_shape=(jax.ShapeDtypeStruct((PACKED, 51...]
    unnamed x4 -> x0, local copies, waits for them, and re-layouts: 1.38 us -> none
where the time goes in v4:
time: 51.9 us; the launch traced here: 51.8 us
  Pallas kernels  51.2 us (99%)
  between operations  0.64 us (1%)
    pallas_call x1, Pallas kernels, camera_update(): pl.pallas_call(camera_kernel, out_shape=(jax.ShapeDtypeStruct((PACKED, 51...  49.9 us
    pallas_call x1, Pallas kernels, point_update(): pl.pallas_call(point_kernel, out_shape=(jax.ShapeDtypeStruct((PACKED, 512...  1.34 us

profile of v4, /device:TPU:1, one launch (start us, length us, event | category | flops | bytes accessed | tf_op | source)
XLA Modules:
  0.0 51.8 jit_solution(1573067381538013727)
XLA Ops:
  0.6 49.9 %marginalize_and_sum.1 = (f32[45,512]{1,0:T(8,128)S(1)}, f32[8,40,128]{2,1,0:T(8,128)S(1)}, bf16[256,3072]{1,0:T(8,128)(2,1)S(1)}, f32[3,27,8,128]{3,2,1,0:T(8,1...) custom-call(f32[384,9,8,128]{3,2,1,0:T(8,128)} %bitcast.4, f32[384,3,8,128]{3,2,1,0:T(8,128)} %bitcast.5, ...), custom_call_target="tpu_custom_call" | custom-call | tf_op jit(solution)/shard_map/marginalize_and_sum/pallas_call | solution.py:408
  50.5 1.3 %point_update.1 = (f32[45,512]{1,0:T(8,128)}, f32[9,512]{1,0:T(8,128)}, f32[3,384]{1,0:T(4,128)}) custom-call(f32[45,512]{1,0:T(8,128)S(1)} %get-tuple-element.9.fac, f32[8,40,128]{2,1,0:T(8,128)S(1)} %get-tuple-element.10.steps, bf16[256,3072]{1,0:T(8,128)(2,1)S(1)} %get-tuple-element.11.pick, s32[1,3072]{1,0:T(1,128)S(1)} %get-tuple-element.12.cam, ...), custom_call_target="tpu_custom_call" | custom-call | tf_op jit(solution)/shard_map/point_update/pallas_call | solution.py:492

commit v5 on v4

--- a/solution.py
+++ b/solution.py
@@ -110,12 +110,16 @@
     count_copy = pltpu.make_async_copy(cnt_hbm, cnt, sem.at[NB, 0])
     cam_copy = pltpu.make_async_copy(cam_hbm, cam, sem.at[NB, 1])
     count_copy.start()
+    cam_copy.start()
     for which in range(3):
         for b in range(NB):
             copy(b, which).start()
-        if which == 0:
-            cam_copy.start()
     count_copy.wait()
+    cam_copy.wait()
+    for b in range(NB):
+        for k in range(K):
+            cam_out[0:1, (b * K + k) * 128 : (b * K + k + 1) * 128] = cam[k : k + 1, b * 128 : (b + 1) * 128]
+    fill_onehot(cam_out, onehot)
 
     jcf = jcv.reshape(NL * CP * K, 128)
     jpf = jpv.reshape(NL * 3 * K, 128)
@@ -141,7 +145,7 @@
             return tuple(sums)
 
         s00, s01, s02 = [
-            jnp.sum(v, axis=0, keepdims=True) for v in lax.fori_loop(0, K, first, (zero,) * 3)
+            jnp.sum(v, axis=0, keepdims=True) for v in lax.fori_loop(0, K, first, (zero,) * 3, unroll=K)
         ]
         norm0 = jnp.sqrt(s00)
         inv0 = 1.0 / norm0
@@ -161,7 +165,7 @@
             return n1, s12
 
         n11, s12 = [
-            jnp.sum(v, axis=0, keepdims=True) for v in lax.fori_loop(0, K, second, (zero,) * 2)
+            jnp.sum(v, axis=0, keepdims=True) for v in lax.fori_loop(0, K, second, (zero,) * 2, unroll=K)
         ]
         norm1 = jnp.sqrt(n11)
         inv1 = 1.0 / norm1
@@ -180,7 +184,7 @@
                 n2 = n2 + rem * rem
             return n2
 
-        n22 = jnp.sum(lax.fori_loop(0, K, third, zero), axis=0, keepdims=True)
+        n22 = jnp.sum(lax.fori_loop(0, K, third, zero, unroll=K), axis=0, keepdims=True)
         norm2 = jnp.sqrt(n22)
         inv2 = 1.0 / norm2
         for n, v in enumerate((inv0, inv1, inv2, r01, r02, r12)):
@@ -223,7 +227,7 @@
             products(b, 2 * h + 1, tb)
             return 0
 
-        lax.fori_loop(0, K // 2, two, 0)
+        lax.fori_loop(0, K // 2, two, 0, unroll=2)
 
         def entry(n):
             v = acc[n, pl.ds(0, 8, stride=8), :]
@@ -261,25 +265,21 @@
         return 0
 
     lax.fori_loop(0, NB, camera_phase, 0)
-    cam_copy.wait()
-    for b in range(NB):
-        for k in range(K):
-            cam_out[0:1, (b * K + k) * 128 : (b * K + k + 1) * 128] = cam[k : k + 1, b * 128 : (b + 1) * 128]
-
-    fill_onehot(cam_out, onehot)
-
-    def sums_of(owner):
-        for half in range(2):
-            for t in range(6):
-                cols = slice(t * 512, (t + 1) * 512)
-                hit = (cam_out[0:1, cols] >> 8) == owner * 2 + half
-                mask = jnp.broadcast_to(hit.astype(f32), (16, 512)).astype(bf16)
-                mask = jnp.concatenate([mask] * 7, axis=0)
-                lhs[half * 112 : (half + 1) * 112, cols] = rec[:, cols] * mask
+
+    def sums_of(owners):
+        for n, owner in enumerate(owners):
+            for half in range(2):
+                rows = slice((n * 2 + half) * 112, (n * 2 + half + 1) * 112)
+                for t in range(6):
+                    cols = slice(t * 512, (t + 1) * 512)
+                    hit = (cam_out[0:1, cols] >> 8) == owner * 2 + half
+                    mask = jnp.broadcast_to(hit.astype(f32), (16, 512)).astype(bf16)
+                    mask = jnp.concatenate([mask] * 7, axis=0)
+                    lhs[rows, cols] = rec[:, cols] * mask
         r = lax.dot_general(
             lhs[...], onehot[...], (((1,), (1,)), ((), ())), preferred_element_type=f32
         )
-        return [r[112 * h : 112 * h + 56] + r[112 * h + 56 : 112 * h + 112] for h in range(2)]
+        return [r[112 * h : 112 * h + 56] + r[112 * h + 56 : 112 * h + 112] for h in range(4)]
 
     ORDER = (2, 1, 3, 0)
 
@@ -290,11 +290,13 @@
             device_id=(img, y * 2 + 1 - core), device_id_type=MESH,
         )
 
-    def other_core(d):
-        sums = sums_of(((y + ORDER[d]) % 4) * 2 + 1 - core)
+    def both_cores(d):
+        to_y = (y + ORDER[d]) % 4
+        sums = sums_of((to_y * 2 + 1 - core, to_y * 2 + core))
         for h in range(2):
             for r in range(7):
                 away[d, h * 7 + r] = sums[h][8 * r : 8 * r + 8]
+                home[d, h * 7 + r] = sums[2 + h][8 * r : 8 * r + 8]
         core_copy(d).start()
 
     def slice_copy(d, q):
@@ -305,12 +307,9 @@
             device_id=(plane(q), ((y + ORDER[d]) % 4) * 2 + core), device_id_type=MESH,
         )
 
-    def own_core(d):
-        sums = sums_of(((y + ORDER[d]) % 4) * 2 + core)
+    def send_on(d):
         core_copy(d).wait_recv()
-        for h in range(2):
-            for r in range(7):
-                home[d, h * 7 + r] = sums[h][8 * r : 8 * r + 8] + from_core[d, h * 7 + r]
+        home[d, 0:OWNERS] = home[d, 0:OWNERS] + from_core[d, 0:OWNERS]
         for q in PLANE:
             if ORDER[d] or q != (0, 0):
                 @pl.when(plane(q) < OWNERS)
@@ -318,14 +317,11 @@
                     slice_copy(d, q).start()
 
     pl.semaphore_wait(barrier, 67)
-    other_core(0)
-    other_core(1)
-    own_core(0)
-    other_core(2)
-    own_core(1)
-    other_core(3)
-    own_core(2)
-    own_core(3)
+    both_cores(0)
+    for d in range(1, 4):
+        both_cores(d)
+        send_on(d - 1)
+    send_on(3)
 
     def sum_copy(q):
         n = q[0] * 4 + q[1]
@@ -431,7 +427,7 @@
             pltpu.VMEM((2 * ROWS, NOBS), bf16),
             pltpu.VMEM((ROWS * 8, 128), f32),
             pltpu.VMEM((256, NOBS), bf16),
-            pltpu.VMEM((224, NOBS), bf16),
+            pltpu.VMEM((448, NOBS), bf16),
             pltpu.VMEM((4, 16, 8, 256), f32),
             pltpu.VMEM((4, 16, 8, 256), f32),
             pltpu.VMEM((4, 16, 8, 256), f32),

time: 51.9 us -> 50.5 us (0.973)
  Pallas kernels: 51.2 us -> 49.7 us
    pallas_call x1, Pallas kernels: 49.9 us -> 48.4 us  [camera_update(): pl.pallas_call(camera_kernel, out_shape=(jax.ShapeDtypeStruct((PACKED, 51...]
where the time goes in v5:
time: 50.5 us; the launch traced here: 50.4 us
  Pallas kernels  49.7 us (98%)
  between operations  0.64 us (1%)
    pallas_call x1, Pallas kernels, camera_update(): pl.pallas_call(camera_kernel, out_shape=(jax.ShapeDtypeStruct((PACKED, 51...  48.4 us
    pallas_call x1, Pallas kernels, point_update(): pl.pallas_call(point_kernel, out_shape=(jax.ShapeDtypeStruct((PACKED, 512...  1.34 us

profile of v5, /device:TPU:1, one launch (start us, length us, event | category | flops | bytes accessed | tf_op | source)
XLA Modules:
  0.0 50.4 jit_solution(16766342616257530853)
XLA Ops:
  0.6 48.4 %marginalize_and_sum.1 = (f32[45,512]{1,0:T(8,128)S(1)}, f32[8,40,128]{2,1,0:T(8,128)S(1)}, bf16[256,3072]{1,0:T(8,128)(2,1)S(1)}, f32[3,27,8,128]{3,2,1,0:T(8,1...) custom-call(f32[384,9,8,128]{3,2,1,0:T(8,128)} %bitcast.4, f32[384,3,8,128]{3,2,1,0:T(8,128)} %bitcast.5, ...), custom_call_target="tpu_custom_call" | custom-call | tf_op jit(solution)/shard_map/marginalize_and_sum/pallas_call | solution.py:404
  49.0 1.3 %point_update.1 = (f32[45,512]{1,0:T(8,128)}, f32[9,512]{1,0:T(8,128)}, f32[3,384]{1,0:T(4,128)}) custom-call(f32[45,512]{1,0:T(8,128)S(1)} %get-tuple-element.9.fac, f32[8,40,128]{2,1,0:T(8,128)S(1)} %get-tuple-element.10.steps, bf16[256,3072]{1,0:T(8,128)(2,1)S(1)} %get-tuple-element.11.pick, s32[1,3072]{1,0:T(1,128)S(1)} %get-tuple-element.12.cam, ...), custom_call_target="tpu_custom_call" | custom-call | tf_op jit(solution)/shard_map/point_update/pallas_call | solution.py:488

commit v6 on v5

--- a/solution.py
+++ b/solution.py
@@ -212,7 +212,7 @@
                     term = held[pair[0]] * held[pair[1]]
                     total[n] = term if total[n] is None else total[n] + term
             for n in range(len(pairs)):
-                acc[base + n, pl.ds(pl.multiple_of(k * 8, 8), 8), :] = total[n]
+                acc[base + n, 8 * k : 8 * k + 8, :] = total[n]
             base += len(pairs)
 
     def camera_phase(b, _):
@@ -220,14 +220,11 @@
         copy(b, 2).wait()
         turn(b, 0, ta)
 
-        def two(h, _):
-            turn(b, 2 * h + 1, tb)
-            products(b, 2 * h, ta)
-            turn(b, jnp.minimum(2 * h + 2, K - 1), ta)
-            products(b, 2 * h + 1, tb)
-            return 0
-
-        lax.fori_loop(0, K // 2, two, 0, unroll=2)
+        for k in range(K):
+            now, later = (ta, tb) if k % 2 == 0 else (tb, ta)
+            if k + 1 < K:
+                turn(b, k + 1, later)
+            products(b, k, now)
 
         def entry(n):
             v = acc[n, pl.ds(0, 8, stride=8), :]

time: 50.5 us -> 49 us (0.970)
  Pallas kernels: 49.7 us -> 48.2 us
    pallas_call x1, Pallas kernels: 48.4 us -> 46.9 us  [camera_update(): pl.pallas_call(camera_kernel, out_shape=(jax.ShapeDtypeStruct((PACKED, 51...]
where the time goes in v6:
time: 49 us; the launch traced here: 48.9 us
  Pallas kernels  48.2 us (98%)
  between operations  0.64 us (1%)
    pallas_call x1, Pallas kernels, camera_update(): pl.pallas_call(camera_kernel, out_shape=(jax.ShapeDtypeStruct((PACKED, 51...  46.9 us
    pallas_call x1, Pallas kernels, point_update(): pl.pallas_call(point_kernel, out_shape=(jax.ShapeDtypeStruct((PACKED, 512...  1.34 us

profile of v6, /device:TPU:1, one launch (start us, length us, event | category | flops | bytes accessed | tf_op | source)
XLA Modules:
  0.0 48.9 jit_solution(12619273971342643216)
XLA Ops:
  0.6 46.9 %marginalize_and_sum.1 = (f32[45,512]{1,0:T(8,128)S(1)}, f32[8,40,128]{2,1,0:T(8,128)S(1)}, bf16[256,3072]{1,0:T(8,128)(2,1)S(1)}, f32[3,27,8,128]{3,2,1,0:T(8,1...) custom-call(f32[384,9,8,128]{3,2,1,0:T(8,128)} %bitcast.4, f32[384,3,8,128]{3,2,1,0:T(8,128)} %bitcast.5, ...), custom_call_target="tpu_custom_call" | custom-call | tf_op jit(solution)/shard_map/marginalize_and_sum/pallas_call | solution.py:401
  47.5 1.3 %point_update.1 = (f32[45,512]{1,0:T(8,128)}, f32[9,512]{1,0:T(8,128)}, f32[3,384]{1,0:T(4,128)}) custom-call(f32[45,512]{1,0:T(8,128)S(1)} %get-tuple-element.9.fac, f32[8,40,128]{2,1,0:T(8,128)S(1)} %get-tuple-element.10.steps, bf16[256,3072]{1,0:T(8,128)(2,1)S(1)} %get-tuple-element.11.pick, s32[1,3072]{1,0:T(1,128)S(1)} %get-tuple-element.12.cam, ...), custom_call_target="tpu_custom_call" | custom-call | tf_op jit(solution)/shard_map/point_update/pallas_call | solution.py:485
